TPU v7x, 512 devices: a whole 4x8x8 slice. The times are simulated.
512 devices in a mesh: replica: 64 (over x, y, core), tensor: 8 (over z).
Axes of the slice: x: 4, y: 8, z: 8, core: 2. Of those that a mesh axis runs over, the one named last changes fastest.
Arguments:
- queries: bfloat16 [8192, 4096], P('replica', 'tensor'), may hold values from -9 to 9
- new_kv: bfloat16 [2, 8192, 1024], P(None, 'replica', 'tensor'), may hold values from -16 to 16
- cache: bfloat16 [512, 2, 64, 1024], P('replica', None, None, 'tensor'), may hold values from -16 to 16
- block_owner: int32 [64, 64], replicated, may hold values from 0 to 63, as said below
- block_slot: int32 [64, 64], replicated, may hold values from 0 to 7, as said below
- prefix_blocks: int32 [64], replicated, may hold values from 1 to 64, 2048 in all
- out_weight: bfloat16 [4096, 4096], P('tensor'), may hold values from -0.09375 to 0.09375
Outputs:
- mixed: bfloat16 [8192, 4096], P(('replica', 'tensor'))
Inputs may be any that keep to these rules, and one draw needn't show every extreme that they name: `block_owner`: within one replica's row, every owner that appears does so exactly 2 times. `block_slot`: the 2 entries of one replica's row that name one owner name different slots. `prefix_blocks`: the largest is 64 in every draw.
All inputs are finite; a program needn't handle non-finite values.
Results may differ from a plain program's by a relative error of at most 0.024.
Values may be sent and summed in bfloat16 or wider, within the bound.
No kernel may reach another device: no remote copies, remote signals or barrier semaphores. Data moves between devices by JAX's collectives and lax.ppermute only.
A program may use at most 64 MiB of HBM per device.

v0:
```python
import jax
import jax.numpy as jnp
from jax import lax
from jax.sharding import PartitionSpec as P

HQ = 32
KVH = 8
HD = 128
BLOCK = 64
MAXB = 64


NEGATIVE = -1e30


def tile_update(softmax_state, query_heads, key_rows, value_rows, allowed, scaling):
    running, totals, weighted = softmax_state
    scores = (
        jnp.einsum("tkgd,skd->kgts", query_heads, key_rows, preferred_element_type=jnp.float32)
        * scaling
    )
    scores = jnp.where(allowed, scores, NEGATIVE)
    fresh = jnp.maximum(running, jnp.max(scores, axis=3))
    weights = jnp.where(allowed, jnp.exp(scores - fresh[..., None]), 0.0)
    factor = jnp.exp(running - fresh)
    totals = totals * factor + jnp.sum(weights, axis=3)
    increment = jnp.einsum(
        "kgts,skd->tkgd",
        weights.astype(jnp.bfloat16),
        value_rows,
        preferred_element_type=jnp.float32,
    )
    weighted = weighted * jnp.transpose(factor, (2, 0, 1))[..., None] + increment
    return (fresh, totals, weighted)


def fold_range(
    softmax_state, query_heads, key_rows, value_rows, lower_key, upper_key, key_span, scaling
):
    tile_first = lower_key // key_span
    tile_last = (upper_key + key_span - 1) // key_span

    def advance(position, carried):
        offset = position * key_span
        key_tile = lax.dynamic_slice_in_dim(key_rows, offset, key_span, 0)
        value_tile = lax.dynamic_slice_in_dim(value_rows, offset, key_span, 0)
        places = offset + jnp.arange(key_span, dtype=jnp.int32)
        allowed = ((places >= lower_key) & (places < upper_key))[None, None, None, :]
        return tile_update(carried, query_heads, key_tile, value_tile, allowed, scaling)

    return lax.fori_loop(tile_first, tile_last, advance, softmax_state)


def fold_blocks(
    softmax_state, query_heads, arrived, positions, lower_block, upper_block, key_span, scaling
):
    chosen = arrived[positions]
    block_len = chosen.shape[2]
    key_count = chosen.shape[0] * block_len
    heads_kv = query_heads.shape[1]
    key_rows = chosen[:, 0].reshape(key_count, heads_kv, -1)
    value_rows = chosen[:, 1].reshape(key_count, heads_kv, -1)
    return fold_range(
        softmax_state,
        query_heads,
        key_rows,
        value_rows,
        lower_block * block_len,
        upper_block * block_len,
        key_span,
        scaling,
    )


def suffix_pass(softmax_state, query_heads, new_keys, new_values, key_span, scaling):
    key_count = new_keys.shape[0]
    row_ids = jnp.arange(key_count, dtype=jnp.int32)
    columns = 0 + jnp.arange(key_span, dtype=jnp.int32)
    allowed = (row_ids[:, None] >= columns[None, :])[None, None]
    softmax_state = tile_update(softmax_state, query_heads, new_keys, new_values, allowed, scaling)
    return softmax_state


def send_table(owner_rows, slot_rows, lower, upper, own_index, capacity):
    places = jnp.arange(owner_rows.shape[1], dtype=jnp.int32)
    chosen = (
        (owner_rows == own_index)
        & (places[None, :] >= lower[:, None])
        & (places[None, :] < upper[:, None])
    )
    ranks = jnp.cumsum(chosen.astype(jnp.int32), axis=1) - 1
    levels = jnp.arange(capacity, dtype=jnp.int32)
    matches = chosen[:, None, :] & (ranks[:, None, :] == levels[None, :, None])
    return jnp.sum(jnp.where(matches, slot_rows[:, None, :] + 1, 0), axis=2)


def receive_index(owner_row, lower, upper, capacity, lane, lane_count):
    places = jnp.arange(owner_row.shape[0], dtype=jnp.int32)
    chosen = (places >= lower) & (places < upper)
    same_owner = owner_row[:, None] == owner_row[None, :]
    earlier = places[None, :] < places[:, None]
    ranks = jnp.sum((same_owner & earlier & chosen[None, :]).astype(jnp.int32), axis=1)
    spots = owner_row * (capacity * lane_count) + lane * capacity + ranks
    return jnp.where(chosen, spots, 0)


def local(queries, new_kv, cache, block_owner, block_slot, prefix_blocks, out_weight):
    replicas = lax.axis_size("replica")
    own_index = lax.axis_index("replica")
    capacity = max(2, MAXB // replicas)
    tokens = queries.shape[0]
    heads_kv = cache.shape[3] // HD
    per_group = HQ // KVH
    scaling = HD ** (-0.5)
    key_span = min(512, MAXB // 2 * BLOCK)
    query_heads = queries.reshape(tokens, heads_kv, per_group, HD)
    new_keys = new_kv[0].reshape(tokens, heads_kv, HD)
    new_values = new_kv[1].reshape(tokens, heads_kv, HD)
    blank_state = (
        jnp.full((heads_kv, per_group, tokens), NEGATIVE, jnp.float32),
        jnp.zeros((heads_kv, per_group, tokens), jnp.float32),
        jnp.zeros((tokens, heads_kv, per_group, HD), jnp.float32),
    )
    nothing = jnp.zeros((), jnp.int32)
    own_row = lax.dynamic_index_in_dim(block_owner, own_index, 0, keepdims=False)
    own_length = lax.dynamic_index_in_dim(prefix_blocks, own_index, 0, keepdims=False)
    slot_table = send_table(
        block_owner, block_slot, jnp.zeros_like(prefix_blocks), prefix_blocks, own_index, capacity
    )[:, None]
    lane_count = 1
    keep_index = receive_index(own_row, nothing, own_length, capacity, 0, lane_count)
    requested = slot_table.reshape(-1)
    picked = cache[jnp.maximum(requested - 1, 0)]
    picked = picked.reshape((replicas, lane_count * capacity) + cache.shape[1:])
    arrived = lax.all_to_all(picked, "replica", split_axis=0, concat_axis=0, tiled=True)
    arrived = arrived.reshape((replicas * lane_count * capacity,) + cache.shape[1:])
    softmax_state = suffix_pass(
        blank_state, query_heads, new_keys, new_values, min(512, tokens), scaling
    )
    softmax_state = fold_blocks(
        softmax_state, query_heads, arrived, keep_index, nothing, own_length, key_span, scaling
    )
    attention = softmax_state[2] / jnp.transpose(softmax_state[1], (2, 0, 1))[..., None]
    attention = attention.reshape(tokens, heads_kv * per_group * HD).astype(jnp.bfloat16)
    return lax.psum_scatter(
        jnp.dot(attention, out_weight, preferred_element_type=jnp.float32).astype(jnp.bfloat16),
        "tensor",
        scatter_dimension=0,
        tiled=True,
    )


def solution(mesh):
    placed = (
        P("replica", "tensor"),
        P(None, "replica", "tensor"),
        P("replica", None, None, "tensor"),
        P(),
        P(),
        P(),
        P("tensor", None),
    )
    return jax.shard_map(
        local, mesh=mesh, in_specs=placed, out_specs=P(("replica", "tensor"), None), check_vma=False
    )
```

profile of v0, /device:TPU:2, one launch (start us, length us, event | category | flops | bytes accessed | tf_op | source)
XLA Modules:
  0.0 198.7 jit_solution(2913148449188847985)
XLA Ops:
  6.5 0.0 copy-start
  6.5 0.9 fusion.48
  7.4 0.2 reduce_window_sum.11
  7.7 0.8 broadcast_add_fusion
  8.4 0.1 select_reduce_fusion
  8.6 0.1 copy.23
  8.7 0.1 reshape.210
  8.8 0.0 copy-done
  8.8 3.1 %gather_fusion = bf16[128,2,64,128]{3,2,1,0:T(8,128)(2,1)} fusion(bf16[8,2,64,128]{3,2,1,0:T(8,128)(2,1)S(1)} %copy-done, s32[1024]{0:T(1024)S(1)} %pad_clamp_fusion.1), kind=kCustom, calls=%fused_computation | custom fusion | bytes 8389120 | tf_op jit(solution)/shard_map/gather | solution.py:133
  11.9 0.0 copy-start.3
  11.9 0.0 copy-start.1
  11.9 0.0 copy-start.2
  11.9 11.2 %all-to-all-start = ((bf16[64,2,2,64,128]{4,3,2,1,0:T(8,128)(2,1)}), bf16[64,2,2,64,128]{4,3,2,1,0:T(8,128)(2,1)}, u32[]{:S(2)}, u32[]{:S(2)}) async-start(bf16[64,2,2,64,128]{4,3,2,1,0:T(8,128)(2,1)} %bitcast.131), calls=%async_computation | async-start | bytes 8388608 | tf_op jit(solution)/shard_map/all_to_all | solution.py:135
  23.1 0.0 reduce-scatter.2.cloned.1.call-start
  23.1 0.0 copy-done.3
  23.1 0.6 dynamic_slice.14
  24.3 0.0 copy-done.1
  24.3 0.1 copy.24
  24.5 0.0 copy-done.2
  24.5 0.2 fusion.52
  24.7 0.1 fusion.27
  24.8 0.2 fusion.24
  25.0 0.1 copy.25
  25.2 0.1 copy.26
  25.3 0.6 iota_compare_fusion.4
  25.9 0.7 fusion.45
  26.6 0.2 convert_reduce_fusion
  26.8 1.3 fusion.44
  28.1 89.9 %all-to-all-done = bf16[64,2,2,64,128]{4,3,2,1,0:T(8,128)(2,1)} async-done(((bf16[64,2,2,64,128]{4,3,2,1,0:T(8,128)(2,1)}), bf16[64,2,2,64,128]{4,3,2,1,0:T(8,128)(2,1)}, u32[]{:S(2)}, u32[]{:S(2)}) %all-to-all-start) | async-done | bytes 4194336 | tf_op jit(solution)/shard_map/all_to_all | solution.py:135
  117.9 3.1 %gather_fusion.1 = bf16[64,2,64,128]{3,2,1,0:T(8,128)(2,1)S(1)} fusion(bf16[128,2,64,128]{3,2,1,0:T(8,128)(2,1)} %bitcast.31, s32[1024]{0:T(1024)S(1)} %pad_clamp_fusion), kind=kCustom, calls=%fused_computation.1 | custom fusion | bytes 4194560 | tf_op jit(solution)/shard_map/gather | solution.py:57
  121.1 1.6 fusion.51
  122.6 2.8 %while.14 = (s32[]{:T(128)}, f32[1,4,128]{2,1,0:T(4,128)S(1)}, f32[1,4,128]{2,1,0:T(4,128)S(1)}, f32[128,1,4,128]{0,3,2,1:T(8,128)S(1)}, s32[]{:T(128)}, /*index...) while((s32[]{:T(128)}, f32[1,4,128]{2,1,0:T(4,128)S(1)}, ...), condition=%wide.region_8.9_spmd, body=%wide.region_5.8_spmd.sunk | while | flops 136711680 | bytes 4098235 | solution.py:51
  122.6 1.2 fusion.66
  123.9 1.3 fusion.69
  125.2 0.2 fusion.68
  125.5 3.9 %convolution_convert_fusion = bf16[128,4096]{1,0:T(8,128)(2,1)} fusion(bf16[128,512]{0,1:T(8,128)(2,1)S(1)} %bitcast.137, bf16[512,4096]{1,0:T(8,128)(2,1)} %param.15), kind=kOutput, calls=%fused_computation.31 | convolution fusion | flops 537395200 | bytes 5373952 | tf_op jit(solution)/shard_map/dot_general | solution.py:146
  129.4 0.0 reduce-scatter.2.cloned.1.call-update
  129.4 62.4 %reduce-scatter.2.cloned.1.call-done = bf16[16,4096]{1,0:T(8,128)(2,1)} async-done(((bf16[128,4096]{1,0:T(8,128)(2,1)}), bf16[16,4096]{1,0:T(8,128)(2,1)}) %reduce-scatter.2.cloned.1.call-update) | async-done | bytes 131088 | tf_op jit(solution)/shard_map/reduce_scatter | solution.py:145
  (11 shorter events, 0.1 us)
Async XLA Ops:
  6.5 2.3 %copy-start = (bf16[8,2,64,128]{3,2,1,0:T(8,128)(2,1)S(1)}, bf16[8,2,64,128]{3,2,1,0:T(8,128)(2,1)}, u32[]{:S(2)}) copy-start(bf16[8,2,64,128]{3,2,1,0:T(8,128)(2,1)} %param.11) | copy-start | bytes 786436
  11.9 11.2 %copy-start.3 = (s32[64]{0:T(128)S(1)}, s32[64]{0:T(128)}, u32[]{:S(2)}) copy-start(s32[64]{0:T(128)} %param.14) | copy-start | bytes 772
  11.9 12.4 %copy-start.1 = (bf16[128,512]{1,0:T(8,128)(2,1)S(1)}, bf16[128,512]{1,0:T(8,128)(2,1)}, u32[]{:S(2)}) copy-start(bf16[128,512]{1,0:T(8,128)(2,1)} %param.9) | copy-start | bytes 393220
  11.9 12.6 %copy-start.2 = (bf16[2,128,128]{2,1,0:T(8,128)(2,1)S(1)}, bf16[2,128,128]{2,1,0:T(8,128)(2,1)}, u32[]{:S(2)}) copy-start(bf16[2,128,128]{2,1,0:T(8,128)(2,1)} %param.10) | copy-start | bytes 196612
  11.9 106.0 %all-to-all-start = ((bf16[64,2,2,64,128]{4,3,2,1,0:T(8,128)(2,1)}), bf16[64,2,2,64,128]{4,3,2,1,0:T(8,128)(2,1)}, u32[]{:S(2)}, u32[]{:S(2)}) async-start(bf16[64,2,2,64,128]{4,3,2,1,0:T(8,128)(2,1)} %bitcast.131), calls=%async_computation | async-start | bytes 8388608 | tf_op jit(solution)/shard_map/all_to_all | solution.py:135
  23.1 168.8 %reduce-scatter.2.cloned.1.call-start = ((), (), s32[]{:S(2)}) async-start(), calls=%async_computation.2 | async-start | bytes 1179648 | tf_op jit(solution)/shard_map/reduce_scatter | solution.py:145
Sparse Core Ops, SparseCore 0:
  129.6 62.2 reduce-scatter.1
where the time goes:
time: 199 us
  waiting for transfers between devices  152 us (76%)
  between operations  14.2 us (7%)
  starting transfers between devices  11.2 us (6%)
  local copies, waits for them, and re-layouts  9.68 us (5%)
  matrix products  6.88 us (3%)
  other arithmetic  4.43 us (2%)
    all_to_all x1, waiting for transfers between devices, local(): lax.all_to_all(picked, 'replica', split_axis=0, concat_axis=0, tiled=True)  89.9 us
    reduce_scatter x1, waiting for transfers between devices, local(): lax.psum_scatter(jnp.dot(attention, out_weight, preferred_element_type=jn...  62.4 us
    all_to_all x1, starting transfers between devices, local(): lax.all_to_all(picked, 'replica', split_axis=0, concat_axis=0, tiled=True)  11.2 us
  transfers between devices with their start and end apart: 2, of which 2 were waited for; matrix products, arithmetic and copies ran while one was open for 2% of the time, Pallas kernels for 0%

commit v1 on v0

v1 whole, which is shorter than its diff:
```python
import math

import jax
import jax.numpy as jnp
from jax import lax
from jax.experimental import pallas as pl
from jax.experimental.pallas import tpu as pltpu
from jax.sharding import Mesh, PartitionSpec as P

HQ = 32
KVH = 8
HD = 128
BLOCK = 64
MAXB = 64
NX, NY, NC, NZ = 4, 8, 2, 8
GROUP = NX * NC
PER = HQ // KVH
TOK = 128
ROWS = PER * TOK
SLOTS = 8
CAP = 2
LIST = NY * CAP
TILE = 4
STATS = 16
NEGATIVE = -1e30
LOG2 = HD ** (-0.5) * math.log2(math.e)


def contract(a, b, da, db):
    return lax.dot_general(a, b, (((da,), (db,)), ((), ())), preferred_element_type=jnp.float32)


def attend_kernel(lists, own, queries, new_kv, *rest):
    shards, out, held, peak, total, weighted, sems = rest[:NY], *rest[NY:]
    copies = [pltpu.make_async_copy(shards[s], held.at[pl.ds(s * SLOTS, SLOTS)], sems.at[s]) for s in range(NY)]
    for copy in copies:
        copy.start()
    for copy in copies:
        copy.wait()

    def heads(g):
        q = queries[g]
        return jnp.concatenate([q[:, h * HD:(h + 1) * HD] for h in range(PER)], axis=0)

    def fold(scores, values):
        top = jnp.maximum(peak[...], jnp.max(scores, axis=0, keepdims=True))
        factor = jnp.exp2((peak[...] - top) * LOG2)
        weights = jnp.exp2((scores - top) * LOG2)
        peak[...] = top
        total[...] = total[...] * factor + jnp.sum(weights, axis=0, keepdims=True)
        weighted[...] = weighted[...] * factor + contract(values, weights.astype(jnp.bfloat16), 0, 0)

    def one_replica(g, carry):
        count = lists[g, LIST]
        peak[...] = jnp.full_like(peak, NEGATIVE)
        total[...] = jnp.zeros_like(total)
        weighted[...] = jnp.zeros_like(weighted)

        @pl.when(g == own[0])
        def _():
            scores = contract(new_kv[0], heads(g), 1, 1)
            key = lax.broadcasted_iota(jnp.int32, (TOK, ROWS), 0)
            token = lax.broadcasted_iota(jnp.int32, (TOK, ROWS), 1) % TOK
            fold(jnp.where(key <= token, scores, NEGATIVE), new_kv[1])

        def one_tile(i, carry):
            ids = [lists[g, i * TILE + k] for k in range(TILE)]
            keys = jnp.concatenate([held[b, 0] for b in ids], axis=0)
            values = jnp.concatenate([held[b, 1] for b in ids], axis=0)
            scores = contract(keys, heads(g), 1, 1)
            place = lax.broadcasted_iota(jnp.int32, scores.shape, 0)
            fold(jnp.where(place < (count - i * TILE) * BLOCK, scores, NEGATIVE), values)
            return carry

        lax.fori_loop(0, (count + TILE - 1) // TILE, one_tile, 0)
        filled = total[...] > 0.0
        safe = jnp.where(filled, total[...], 1.0)
        out[g, pl.ds(0, HD), :] = (weighted[...] / safe).astype(jnp.bfloat16)
        level = jnp.where(filled, peak[...] * LOG2 + jnp.log2(safe), NEGATIVE)
        first = level.astype(jnp.bfloat16)
        level = level - first.astype(jnp.float32)
        second = level.astype(jnp.bfloat16)
        third = level - second.astype(jnp.float32)
        row = lax.broadcasted_iota(jnp.int32, (STATS, ROWS), 0)
        stats = jnp.where(row == 0, first.astype(jnp.float32), jnp.where(row == 1, second.astype(jnp.float32), jnp.where(row == 2, third, 0.0)))
        out[g, pl.ds(HD, STATS), :] = stats.astype(jnp.bfloat16)
        return carry

    lax.fori_loop(0, GROUP, one_replica, 0)


def attend(lists, own, queries, new_kv, shards):
    vmem, smem = pl.BlockSpec(memory_space=pltpu.VMEM), pl.BlockSpec(memory_space=pltpu.SMEM)
    return pl.pallas_call(
        attend_kernel,
        out_shape=jax.ShapeDtypeStruct((GROUP, HD + STATS, ROWS), jnp.bfloat16),
        in_specs=[smem, smem, vmem, vmem] + [pl.BlockSpec(memory_space=pl.ANY)] * NY,
        out_specs=vmem,
        scratch_shapes=[
            pltpu.VMEM((NY * SLOTS, 2, BLOCK, HD), jnp.bfloat16),
            pltpu.VMEM((1, ROWS), jnp.float32),
            pltpu.VMEM((1, ROWS), jnp.float32),
            pltpu.VMEM((HD, ROWS), jnp.float32),
            pltpu.SemaphoreType.DMA((NY,)),
        ],
        compiler_params=pltpu.CompilerParams(vmem_limit_bytes=32 << 20),
        name="attend",
    )(lists, own, queries, new_kv, *shards)


def project_kernel(parts, weight, out, attended):
    @pl.when(pl.program_id(0) == 0)
    def _():
        levels = []
        for i in range(GROUP):
            stats = parts[i, pl.ds(HD, STATS), :].astype(jnp.float32)
            levels.append(stats[0:1] + stats[1:2] + stats[2:3])
        top = levels[0]
        for level in levels[1:]:
            top = jnp.maximum(top, level)
        shares = [jnp.exp2(level - top) for level in levels]
        whole = shares[0]
        for share in shares[1:]:
            whole = whole + share
        for h in range(PER):
            columns = pl.ds(h * TOK, TOK)
            mixed = jnp.zeros((HD, TOK), jnp.float32)
            for i in range(GROUP):
                mixed = mixed + parts[i, pl.ds(0, HD), columns].astype(jnp.float32) * (shares[i] / whole)[:, h * TOK:(h + 1) * TOK]
            attended[:, h * HD:(h + 1) * HD] = jnp.transpose(mixed).astype(jnp.bfloat16)

    out[...] = jnp.dot(attended[...], weight[...], preferred_element_type=jnp.float32).astype(jnp.bfloat16)


def project(parts, weight):
    width = weight.shape[1]
    step = 1024
    return pl.pallas_call(
        project_kernel,
        out_shape=jax.ShapeDtypeStruct((TOK, width), jnp.bfloat16),
        grid=(width // step,),
        in_specs=[
            pl.BlockSpec((GROUP, HD + STATS, ROWS), lambda n: (0, 0, 0)),
            pl.BlockSpec((ROWS, step), lambda n: (0, n)),
        ],
        out_specs=pl.BlockSpec((TOK, step), lambda n: (0, n)),
        scratch_shapes=[pltpu.VMEM((TOK, ROWS), jnp.bfloat16)],
        compiler_params=pltpu.CompilerParams(vmem_limit_bytes=32 << 20),
        name="project",
    )(parts, weight)


def block_lists(block_owner, block_slot, prefix_blocks, x, y, c):
    pick = lambda a: lax.dynamic_index_in_dim(a.reshape(NX, NY, NC, -1), y, 1, keepdims=False).reshape(GROUP, -1)
    owners, slots, lengths = pick(block_owner), pick(block_slot), pick(prefix_blocks)
    column = owners // (NY * NC) * NC + owners % NC
    ring = (owners // NC - y) % NY
    places = jnp.arange(MAXB, dtype=jnp.int32)
    mine = (column == x * NC + c) & (places[None, :] < lengths)
    earlier = (places[:, None] <= places[None, :]).astype(jnp.float32)
    ranks = jnp.dot(mine.astype(jnp.float32), earlier).astype(jnp.int32) - 1
    codes = ring * SLOTS + slots
    matches = mine[:, None, :] & (ranks[:, None, :] == jnp.arange(LIST, dtype=jnp.int32)[None, :, None])
    lists = jnp.sum(jnp.where(matches, codes[:, None, :], 0), axis=2)
    counts = jnp.sum(mine.astype(jnp.int32), axis=1, keepdims=True)
    return jnp.concatenate([lists, counts], axis=1)


def local(queries, new_kv, cache, block_owner, block_slot, prefix_blocks, out_weight):
    x, y, c = lax.axis_index("x"), lax.axis_index("y"), lax.axis_index("c")
    gathered = lax.all_gather(queries, ("x", "c"), axis=0)
    up = [(i, (i + 1) % NY) for i in range(NY)]
    down = [(i, (i - 1) % NY) for i in range(NY)]
    shards = [cache] * NY
    below = above = cache
    for step in range(1, NY // 2 + 1):
        below = lax.ppermute(below, "y", up)
        shards[NY - step] = below
        if step < NY // 2:
            above = lax.ppermute(above, "y", down)
            shards[step] = above
    lists = block_lists(block_owner, block_slot, prefix_blocks, x, y, c)
    own = (x * NC + c).reshape(1)
    parts = attend(lists, own, gathered, new_kv, shards)
    parts = lax.all_to_all(parts, ("x", "c"), split_axis=0, concat_axis=0, tiled=True)
    partial = project(parts, out_weight).reshape(NZ, TOK // NZ, -1)
    arrived = lax.all_to_all(partial, "z", split_axis=0, concat_axis=0, tiled=True)
    return jnp.sum(arrived.astype(jnp.float32), axis=0).astype(jnp.bfloat16)


def solution(mesh):
    fine = Mesh(mesh.devices.reshape(NX, NY, NC, NZ), ("x", "y", "c", "z"))
    replica = ("x", "y", "c")
    placed = (
        P(replica, "z"),
        P(None, replica, "z"),
        P(replica, None, None, "z"),
        P(),
        P(),
        P(),
        P("z", None),
    )
    return jax.shard_map(
        local, mesh=fine, in_specs=placed, out_specs=P(("x", "y", "c", "z"), None), check_vma=False
    )
```

time: 199 us -> 128 us (0.64)
  the two profiles are of different devices: /device:TPU:2 before, /device:TPU:32 now
where the time goes in v1:
time: 128 us
  blocking collectives  59.3 us (46%)
  starting transfers between devices  23.5 us (18%)
  waiting for transfers between devices  14.1 us (11%)
  between operations  13.5 us (11%)
  Pallas kernels  10.1 us (8%)
  local copies, waits for them, and re-layouts  5.12 us (4%)
  other arithmetic  2.1 us (2%)
    all_to_all x1, blocking collectives, local(): lax.all_to_all(partial, 'z', split_axis=0, concat_axis=0, tiled=True)  38.7 us
    all_to_all x1, blocking collectives, local(): lax.all_to_all(parts, ('x', 'c'), split_axis=0, concat_axis=0, tiled=True)  20.6 us
    ppermute x3, starting transfers between devices, local(): above = lax.ppermute(above, 'y', down)  15.2 us
    ppermute x4, waiting for transfers between devices, local(): below = lax.ppermute(below, 'y', up)  13.1 us
    ppermute x4, starting transfers between devices, local(): below = lax.ppermute(below, 'y', up)  8.31 us
    pallas_call x1, Pallas kernels, attend(): pl.pallas_call(attend_kernel, out_shape=jax.ShapeDtypeStruct((GROUP, HD +...  8.16 us
    unnamed x10, local copies, waits for them, and re-layouts  3.02 us
  transfers between devices with their start and end apart: 8, of which 5 were waited for; matrix products, arithmetic and copies ran while one was open for 3% of the time, Pallas kernels for 0%

profile of v1, /device:TPU:32, one launch (start us, length us, event | category | flops | bytes accessed | tf_op | source)
XLA Modules:
  0.0 127.9 jit_solution(1567183328428868740)
XLA Ops:
  6.5 0.0 copy-start
  6.5 0.0 all-gather.3.cloned.1.call-start
  6.5 0.7 all-gather.3.cloned.1.call-update
  7.3 2.6 %collective-permute-start.3 = (bf16[8,2,64,128]{3,2,1,0:T(8,128)(2,1)}, bf16[8,2,64,128]{3,2,1,0:T(8,128)(2,1)S(1)}, u32[]{:S(2)}, u32[]{:S(2)}) collective-permute-start(bf16[8,2,64,128]{3,2,1,0:T(8,128)(2,1)} %rest_0_.1), channel_id=1, source_target_pairs={{0,16},{16,32},{32,48},{48,64},{64,80},{80,96},{96,112},{112,0},{1... | collective-permute-start | bytes 786440 | tf_op jit(solution)/shard_map/ppermute | solution.py:177
  9.9 4.5 %collective-permute-start = (bf16[8,2,64,128]{3,2,1,0:T(8,128)(2,1)}, bf16[8,2,64,128]{3,2,1,0:T(8,128)(2,1)S(1)}, u32[]{:S(2)}, u32[]{:S(2)}) collective-permute-start(bf16[8,2,64,128]{3,2,1,0:T(8,128)(2,1)} %rest_0_.1), channel_id=1, source_target_pairs={{0,112},{16,0},{32,16},{48,32},{64,48},{80,64},{96,80},{112,96},{1... | collective-permute-start | bytes 786440 | tf_op jit(solution)/shard_map/ppermute | solution.py:180
  14.3 0.7 reshape.157
  15.1 0.5 broadcast.180
  15.6 0.7 fusion.15
  16.3 2.3 %collective-permute-done.3.rest_7_ = bf16[8,2,64,128]{3,2,1,0:T(8,128)(2,1)S(1)} collective-permute-done((bf16[8,2,64,128]{3,2,1,0:T(8,128)(2,1)}, bf16[8,2,64,128]{3,2,1,0:T(8,128)(2,1)S(1)}, u32[]{:S(2)}, u32[]{:S(2)}) %collective-permute-start.3) | collective-permute-done | bytes 262176 | tf_op jit(solution)/shard_map/ppermute | solution.py:177
  18.6 1.9 %collective-permute-start.4 = (bf16[8,2,64,128]{3,2,1,0:T(8,128)(2,1)S(1)}, bf16[8,2,64,128]{3,2,1,0:T(8,128)(2,1)S(1)}, u32[]{:S(2)}, u32[]{:S(2)}) collective-permute-start(bf16[8,2,64,128]{3,2,1,0:T(8,128)(2,1)S(1)} %collective-permute-done.3.rest_7_), channel_id=1, source_target_pairs={{0,16},{16,32},{32,48},{48,64},{64,80},{80,96},{96,112},{112,0},{1... | collective-permute-start | bytes 786440 | tf_op jit(solution)/shard_map/ppermute | solution.py:177
  20.5 0.9 fusion.11
  21.4 0.1 lt.56
  21.5 0.1 fusion.12
  21.6 0.0 collective-permute-done.rest_1_
  21.6 5.1 %collective-permute-start.1 = (bf16[8,2,64,128]{3,2,1,0:T(8,128)(2,1)S(1)}, bf16[8,2,64,128]{3,2,1,0:T(8,128)(2,1)S(1)}, u32[]{:S(2)}, u32[]{:S(2)}) collective-permute-start(bf16[8,2,64,128]{3,2,1,0:T(8,128)(2,1)S(1)} %collective-permute-done.rest_1_), channel_id=1, source_target_pairs={{0,112},{16,0},{32,16},{48,32},{64,48},{80,64},{96,80},{112,96},{1... | collective-permute-start | bytes 786440 | tf_op jit(solution)/shard_map/ppermute | solution.py:180
  26.7 2.1 %collective-permute-done.4.rest_6_ = bf16[8,2,64,128]{3,2,1,0:T(8,128)(2,1)S(1)} collective-permute-done((bf16[8,2,64,128]{3,2,1,0:T(8,128)(2,1)S(1)}, bf16[8,2,64,128]{3,2,1,0:T(8,128)(2,1)S(1)}, u32[]{:S(2)}, u32[]{:S(2)}) %collective-permute-start.4) | collective-permute-done | bytes 262176 | tf_op jit(solution)/shard_map/ppermute | solution.py:177
  28.9 1.9 %collective-permute-start.5 = (bf16[8,2,64,128]{3,2,1,0:T(8,128)(2,1)S(1)}, bf16[8,2,64,128]{3,2,1,0:T(8,128)(2,1)S(1)}, u32[]{:S(2)}, u32[]{:S(2)}) collective-permute-start(bf16[8,2,64,128]{3,2,1,0:T(8,128)(2,1)S(1)} %collective-permute-done.4.rest_6_), channel_id=1, source_target_pairs={{0,16},{16,32},{32,48},{48,64},{64,80},{80,96},{96,112},{112,0},{1... | collective-permute-start | bytes 786440 | tf_op jit(solution)/shard_map/ppermute | solution.py:177
  30.8 0.0 copy-done
  30.9 0.3 collective-permute-done.1.rest_2_
  31.1 5.6 %collective-permute-start.2 = (bf16[8,2,64,128]{3,2,1,0:T(8,128)(2,1)S(1)}, bf16[8,2,64,128]{3,2,1,0:T(8,128)(2,1)S(1)}, u32[]{:S(2)}, u32[]{:S(2)}) collective-permute-start(bf16[8,2,64,128]{3,2,1,0:T(8,128)(2,1)S(1)} %collective-permute-done.1.rest_2_), channel_id=1, source_target_pairs={{0,112},{16,0},{32,16},{48,32},{64,48},{80,64},{96,80},{112,96},{1... | collective-permute-start | bytes 786440 | tf_op jit(solution)/shard_map/ppermute | solution.py:180
  36.7 1.6 %collective-permute-done.5.rest_5_ = bf16[8,2,64,128]{3,2,1,0:T(8,128)(2,1)S(1)} collective-permute-done((bf16[8,2,64,128]{3,2,1,0:T(8,128)(2,1)S(1)}, bf16[8,2,64,128]{3,2,1,0:T(8,128)(2,1)S(1)}, u32[]{:S(2)}, u32[]{:S(2)}) %collective-permute-start.5) | collective-permute-done | bytes 262176 | tf_op jit(solution)/shard_map/ppermute | solution.py:177
  38.4 1.9 %collective-permute-start.6 = (bf16[8,2,64,128]{3,2,1,0:T(8,128)(2,1)S(1)}, bf16[8,2,64,128]{3,2,1,0:T(8,128)(2,1)S(1)}, u32[]{:S(2)}, u32[]{:S(2)}) collective-permute-start(bf16[8,2,64,128]{3,2,1,0:T(8,128)(2,1)S(1)} %collective-permute-done.5.rest_5_), channel_id=1, source_target_pairs={{0,16},{16,32},{32,48},{48,64},{64,80},{80,96},{96,112},{112,0},{1... | collective-permute-start | bytes 786440 | tf_op jit(solution)/shard_map/ppermute | solution.py:177
  40.3 0.1 fusion
  40.4 0.1 broadcast_in_dim.25
  40.5 0.2 select_reduce_fusion
  40.7 0.1 pad_add_fusion.lists
  40.8 0.0 collective-permute-done.2.rest_3_
  40.8 7.0 %collective-permute-done.6.rest_4_ = bf16[8,2,64,128]{3,2,1,0:T(8,128)(2,1)S(1)} collective-permute-done((bf16[8,2,64,128]{3,2,1,0:T(8,128)(2,1)S(1)}, bf16[8,2,64,128]{3,2,1,0:T(8,128)(2,1)S(1)}, u32[]{:S(2)}, u32[]{:S(2)}) %collective-permute-start.6) | collective-permute-done | bytes 262176 | tf_op jit(solution)/shard_map/ppermute | solution.py:177
  47.8 0.0 all-gather.3.cloned.1.call-done
  47.8 0.0 copy-start.2
  47.8 1.2 copy-done.2
  49.0 0.0 copy-start.3
  49.0 0.9 copy-done.3
  50.0 0.0 copy-start.4
  50.0 0.8 copy-done.4
  50.8 0.0 copy-start.1
  50.8 8.2 %attend.1 = bf16[8,144,512]{2,1,0:T(8,128)(2,1)S(1)} custom-call(s32[8,17]{1,0:T(8,128)S(1)} %pad_add_fusion.lists, s32[1]{0:T(128)} %bitcast.5.own, bf16[8,128,512]{2,1,0:T(8,128)(2,1)S(1)} %bitcast.31, bf16[2,128,128]{2,1,0:T(8,128)(2,1)S(1)} %copy-done.4, bf16[8,2,64,128]{3,2,1,0:T(8,128)(2,1)S(1)} %copy-done.3, ...), custom_call_target="tpu_custom_call" | custom-call | tf_op jit(solution)/shard_map/attend/pallas_call | solution.py:94
  59.0 20.6 %all_to_all.10.parts = bf16[8,144,512]{2,1,0:T(8,128)(2,1)S(1)} all-to-all(bf16[8,144,512]{2,1,0:T(8,128)(2,1)S(1)} %attend.1), channel_id=1, replica_groups=mesh['x'=4,'y'=8,'c'=2,'z'=8] {'x','c'}, dimensions={0} | all-to-all | bytes 2359296 | tf_op jit(solution)/shard_map/all_to_all | solution.py:185
  79.6 0.0 copy-done.1
  79.6 2.0 %project.1 = bf16[128,4096]{1,0:T(8,128)(2,1)S(1)} custom-call(bf16[8,144,512]{2,1,0:T(8,128)(2,1)S(1)} %all_to_all.10.parts, bf16[512,4096]{1,0:T(8,128)(2,1)S(1)} %copy-done.1), custom_call_target="tpu_custom_call" | custom-call | tf_op jit(solution)/shard_map/project/pallas_call | solution.py:138
  81.6 38.7 %all_to_all.11 = bf16[8,16,4096]{2,1,0:T(8,128)(2,1)S(1)} all-to-all(bf16[8,16,4096]{2,1,0:T(8,128)(2,1)S(1)} %bitcast.30), channel_id=1, replica_groups=mesh['x'=4,'y'=8,'c'=2,'z'=8] {'z'}, dimensions={0} | all-to-all | bytes 2097152 | tf_op jit(solution)/shard_map/all_to_all | solution.py:187
  120.3 0.8 reduce_sum.32
  (2 shorter events, 0.0 us)
Async XLA Ops:
  6.5 24.3 %copy-start = (s32[64,64]{1,0:T(8,128)S(1)}, s32[64,64]{1,0:T(8,128)}, u32[]{:S(2)}) copy-start(s32[64,64]{1,0:T(8,128)} %param.11) | copy-start | bytes 49156
  6.5 41.3 %all-gather.3.cloned.1.call-start = ((), (), s32[]{:S(2)}) async-start(), calls=%async_computation.2 | async-start | bytes 1179648 | tf_op jit(solution)/shard_map/all_gather | solution.py:171
  7.3 11.4 %collective-permute-start.3 = (bf16[8,2,64,128]{3,2,1,0:T(8,128)(2,1)}, bf16[8,2,64,128]{3,2,1,0:T(8,128)(2,1)S(1)}, u32[]{:S(2)}, u32[]{:S(2)}) collective-permute-start(bf16[8,2,64,128]{3,2,1,0:T(8,128)(2,1)} %rest_0_.1), channel_id=1, source_target_pairs={{0,16},{16,32},{32,48},{48,64},{64,80},{80,96},{96,112},{112,0},{1... | collective-permute-start | bytes 786440 | tf_op jit(solution)/shard_map/ppermute | solution.py:177
  9.9 11.8 %collective-permute-start = (bf16[8,2,64,128]{3,2,1,0:T(8,128)(2,1)}, bf16[8,2,64,128]{3,2,1,0:T(8,128)(2,1)S(1)}, u32[]{:S(2)}, u32[]{:S(2)}) collective-permute-start(bf16[8,2,64,128]{3,2,1,0:T(8,128)(2,1)} %rest_0_.1), channel_id=1, source_target_pairs={{0,112},{16,0},{32,16},{48,32},{64,48},{80,64},{96,80},{112,96},{1... | collective-permute-start | bytes 786440 | tf_op jit(solution)/shard_map/ppermute | solution.py:180
  18.6 10.3 %collective-permute-start.4 = (bf16[8,2,64,128]{3,2,1,0:T(8,128)(2,1)S(1)}, bf16[8,2,64,128]{3,2,1,0:T(8,128)(2,1)S(1)}, u32[]{:S(2)}, u32[]{:S(2)}) collective-permute-start(bf16[8,2,64,128]{3,2,1,0:T(8,128)(2,1)S(1)} %collective-permute-done.3.rest_7_), channel_id=1, source_target_pairs={{0,16},{16,32},{32,48},{48,64},{64,80},{80,96},{96,112},{112,0},{1... | collective-permute-start | bytes 786440 | tf_op jit(solution)/shard_map/ppermute | solution.py:177
  21.6 9.5 %collective-permute-start.1 = (bf16[8,2,64,128]{3,2,1,0:T(8,128)(2,1)S(1)}, bf16[8,2,64,128]{3,2,1,0:T(8,128)(2,1)S(1)}, u32[]{:S(2)}, u32[]{:S(2)}) collective-permute-start(bf16[8,2,64,128]{3,2,1,0:T(8,128)(2,1)S(1)} %collective-permute-done.rest_1_), channel_id=1, source_target_pairs={{0,112},{16,0},{32,16},{48,32},{64,48},{80,64},{96,80},{112,96},{1... | collective-permute-start | bytes 786440 | tf_op jit(solution)/shard_map/ppermute | solution.py:180
  28.9 9.5 %collective-permute-start.5 = (bf16[8,2,64,128]{3,2,1,0:T(8,128)(2,1)S(1)}, bf16[8,2,64,128]{3,2,1,0:T(8,128)(2,1)S(1)}, u32[]{:S(2)}, u32[]{:S(2)}) collective-permute-start(bf16[8,2,64,128]{3,2,1,0:T(8,128)(2,1)S(1)} %collective-permute-done.4.rest_6_), channel_id=1, source_target_pairs={{0,16},{16,32},{32,48},{48,64},{64,80},{80,96},{96,112},{112,0},{1... | collective-permute-start | bytes 786440 | tf_op jit(solution)/shard_map/ppermute | solution.py:177
  31.1 9.6 %collective-permute-start.2 = (bf16[8,2,64,128]{3,2,1,0:T(8,128)(2,1)S(1)}, bf16[8,2,64,128]{3,2,1,0:T(8,128)(2,1)S(1)}, u32[]{:S(2)}, u32[]{:S(2)}) collective-permute-start(bf16[8,2,64,128]{3,2,1,0:T(8,128)(2,1)S(1)} %collective-permute-done.1.rest_2_), channel_id=1, source_target_pairs={{0,112},{16,0},{32,16},{48,32},{64,48},{80,64},{96,80},{112,96},{1... | collective-permute-start | bytes 786440 | tf_op jit(solution)/shard_map/ppermute | solution.py:180
  38.4 9.5 %collective-permute-start.6 = (bf16[8,2,64,128]{3,2,1,0:T(8,128)(2,1)S(1)}, bf16[8,2,64,128]{3,2,1,0:T(8,128)(2,1)S(1)}, u32[]{:S(2)}, u32[]{:S(2)}) collective-permute-start(bf16[8,2,64,128]{3,2,1,0:T(8,128)(2,1)S(1)} %collective-permute-done.5.rest_5_), channel_id=1, source_target_pairs={{0,16},{16,32},{32,48},{48,64},{64,80},{80,96},{96,112},{112,0},{1... | collective-permute-start | bytes 786440 | tf_op jit(solution)/shard_map/ppermute | solution.py:177
  47.8 1.2 copy-start.2
  49.0 0.9 copy-start.3
  50.0 0.8 copy-start.4
  50.8 28.8 %copy-start.1 = (bf16[512,4096]{1,0:T(8,128)(2,1)S(1)}, bf16[512,4096]{1,0:T(8,128)(2,1)}, u32[]{:S(2)}) copy-start(bf16[512,4096]{1,0:T(8,128)(2,1)} %weight.1) | copy-start | bytes 12582916
Sparse Core Ops, SparseCore 0:
  9.5 32.9 all-gather.2

commit v2 on v1

v2 whole, which is shorter than its diff:
```python
import math

import jax
import jax.numpy as jnp
from jax import lax
from jax.experimental import pallas as pl
from jax.experimental.pallas import tpu as pltpu
from jax.sharding import Mesh, PartitionSpec as P

HQ = 32
KVH = 8
HD = 128
BLOCK = 64
MAXB = 64
NX, NY, NC, NZ = 4, 8, 2, 8
GROUP = NX * NC
PER = HQ // KVH
TOK = 128
ROWS = PER * TOK
SLOTS = 8
CAP = 2
LIST = NY * CAP
TILE = 4
PAIR = 2
STATS = 16
NEGATIVE = -1e30
FLOOR = -1e29
LOG2 = HD ** (-0.5) * math.log2(math.e)


def contract(a, b, da, db):
    return lax.dot_general(a, b, (((da,), (db,)), ((), ())), preferred_element_type=jnp.float32)


def lists_kernel(x, y, c, lengths, owners, slots, lists):
    rows = [(g // NC * NY + y[0]) * NC + g % NC for g in range(GROUP)]
    owner = jnp.concatenate([owners[pl.ds(r, 1), :] for r in rows], axis=0)
    slot = jnp.concatenate([slots[pl.ds(r, 1), :] for r in rows], axis=0)
    length = jnp.concatenate([jnp.full((1, MAXB), lengths[r], jnp.int32) for r in rows], axis=0)
    place = lax.broadcasted_iota(jnp.int32, (GROUP, MAXB), 1)
    mine = (owner // (NY * NC) == x[0]) & (owner % NC == c[0]) & (place < length)
    code = ((owner // NC - y[0]) * (1 - 2 * c[0]) + 2 * NY) % NY * SLOTS + slot
    earlier = lax.broadcasted_iota(jnp.int32, (MAXB, MAXB), 0) < lax.broadcasted_iota(jnp.int32, (MAXB, MAXB), 1)
    flags = mine.astype(jnp.float32)
    ranks = jnp.dot(flags, earlier.astype(jnp.float32), preferred_element_type=jnp.float32)
    lane = lax.broadcasted_iota(jnp.int32, (GROUP, HD), 1)
    table = jnp.where(lane == LIST, jnp.sum(flags, axis=1, keepdims=True), 0.0)
    code = jnp.where(mine, code.astype(jnp.float32), 0.0)
    for k in range(LIST):
        entry = jnp.sum(jnp.where(ranks == k, code, 0.0), axis=1, keepdims=True)
        table = jnp.where(lane == k, entry, table)
    lists[...] = table.astype(jnp.int32)


def block_lists(x, y, c, lengths, owners, slots):
    vmem, smem = pl.BlockSpec(memory_space=pltpu.VMEM), pl.BlockSpec(memory_space=pltpu.SMEM)
    return pl.pallas_call(
        lists_kernel,
        out_shape=pltpu.VMEM((GROUP, HD), jnp.int32),
        in_specs=[smem] * 4 + [vmem] * 2,
        out_specs=vmem,
        compiler_params=pltpu.CompilerParams(vmem_limit_bytes=4 << 20),
        name="block_lists",
    )(x, y, c, lengths, *(pltpu.with_memory_space_constraint(a, pltpu.HBM) for a in (owners, slots)))


def attend_kernel(x, c, lists, new_kv, *rest):
    shards, asked, rest = rest[:NY], rest[NY:NY + NC], rest[NY + NC:]
    out, queries, fresh, held, peak, total, weighted, sems = rest
    first = [pltpu.make_async_copy(asked[d], queries.at[d], sems.at[NY + d]) for d in range(NC)]
    first.append(pltpu.make_async_copy(new_kv, fresh, sems.at[NY + NC]))
    later = [pltpu.make_async_copy(shards[s], held.at[pl.ds(s * SLOTS, SLOTS)], sems.at[s]) for s in range(NY)]
    for copy in first + later:
        copy.start()
    own = x[0] * NC + c[0]

    def heads(g):
        q = queries[(g + c[0]) % NC, g // NC]
        return jnp.concatenate([q[:, h * HD:(h + 1) * HD] for h in range(PER)], axis=0)

    def fold(p, scores, values):
        top = jnp.maximum(peak[p], jnp.max(scores, axis=0, keepdims=True))
        factor = jnp.exp2((peak[p] - top) * LOG2)
        weights = jnp.exp2((scores - top) * LOG2)
        peak[p] = top
        total[p] = total[p] * factor + jnp.sum(weights, axis=0, keepdims=True)
        weighted[p] = weighted[p] * factor + contract(values, weights.astype(jnp.bfloat16), 0, 0)

    def reset(p):
        peak[p] = jnp.full((1, ROWS), FLOOR, jnp.float32)
        total[p] = jnp.zeros((1, ROWS), jnp.float32)
        weighted[p] = jnp.zeros((HD, ROWS), jnp.float32)

    reset(0)
    for copy in first:
        copy.wait()
    scores = contract(fresh[0], heads(own), 1, 1)
    key = lax.broadcasted_iota(jnp.int32, (TOK, ROWS), 0)
    token = lax.broadcasted_iota(jnp.int32, (TOK, ROWS), 1) % TOK
    fold(0, jnp.where(key <= token, scores, NEGATIVE), fresh[1])
    for copy in later:
        copy.wait()

    def finish(p, g):
        filled = total[p] > 0.0
        safe = jnp.where(filled, total[p], 1.0)
        level = jnp.where(filled, peak[p] * LOG2 + jnp.log2(safe), NEGATIVE)
        high = level.astype(jnp.bfloat16).astype(jnp.float32)
        middle = (level - high).astype(jnp.bfloat16).astype(jnp.float32)
        row = lax.broadcasted_iota(jnp.int32, (STATS, ROWS), 0)
        stats = jnp.where(row == 0, high, jnp.where(row == 1, middle, jnp.where(row == 2, level - high - middle, 0.0)))
        out[g, pl.ds(0, HD), :] = (weighted[p] * (1.0 / safe)).astype(jnp.bfloat16)
        out[g, pl.ds(HD, STATS), :] = stats.astype(jnp.bfloat16)

    def one_pair(i, carry):
        pair = [(own + i * PAIR + p) % GROUP for p in range(PAIR)]
        counts = [lists[g, LIST] for g in pair]
        for p in range(PAIR):
            if p:
                reset(p)
            else:
                pl.when(i > 0)(lambda: reset(0))

        def one_tile(j, carry):
            loaded = []
            for g, count in zip(pair, counts):
                ids = [lists[g, j * TILE + k] for k in range(TILE)]
                keys = jnp.concatenate([held[b, 0] for b in ids], axis=0)
                values = jnp.concatenate([held[b, 1] for b in ids], axis=0)
                scores = contract(keys, heads(g), 1, 1)
                place = lax.broadcasted_iota(jnp.int32, scores.shape, 0)
                loaded.append((jnp.where(place < (count - j * TILE) * BLOCK, scores, NEGATIVE), values))
            for p, (scores, values) in enumerate(loaded):
                fold(p, scores, values)
            return carry

        longest = counts[0]
        for count in counts[1:]:
            longest = jnp.maximum(longest, count)
        lax.fori_loop(0, (longest + TILE - 1) // TILE, one_tile, 0)
        for p, g in enumerate(pair):
            finish(p, g)
        return carry

    lax.fori_loop(0, GROUP // PAIR, one_pair, 0)


def attend(x, c, lists, new_kv, asked, shards):
    vmem, smem, free = (pl.BlockSpec(memory_space=m) for m in (pltpu.VMEM, pltpu.SMEM, pl.ANY))
    new_kv, own = (pltpu.with_memory_space_constraint(a, pltpu.HBM) for a in (new_kv, shards[0]))
    return pl.pallas_call(
        attend_kernel,
        out_shape=jax.ShapeDtypeStruct((GROUP, HD + STATS, ROWS), jnp.bfloat16),
        in_specs=[smem, smem, smem] + [free] * (1 + NC + NY),
        out_specs=vmem,
        scratch_shapes=[
            pltpu.VMEM((NC, NX, TOK, ROWS), jnp.bfloat16),
            pltpu.VMEM((2, TOK, HD), jnp.bfloat16),
            pltpu.VMEM((NY * SLOTS, 2, BLOCK, HD), jnp.bfloat16),
            pltpu.VMEM((PAIR, 1, ROWS), jnp.float32),
            pltpu.VMEM((PAIR, 1, ROWS), jnp.float32),
            pltpu.VMEM((PAIR, HD, ROWS), jnp.float32),
            pltpu.SemaphoreType.DMA((NY + NC + 1,)),
        ],
        compiler_params=pltpu.CompilerParams(vmem_limit_bytes=16 << 20),
        name="attend",
    )(x, c, lists, new_kv, own, *shards[1:], *asked)


def project_kernel(parts, weight, out, attended):
    @pl.when(pl.program_id(0) == 0)
    def _():
        levels = []
        for i in range(GROUP):
            stats = parts[i, pl.ds(HD, STATS), :].astype(jnp.float32)
            levels.append(stats[0:1] + stats[1:2] + stats[2:3])
        top = levels[0]
        for level in levels[1:]:
            top = jnp.maximum(top, level)
        shares = [jnp.exp2(level - top) for level in levels]
        whole = shares[0]
        for share in shares[1:]:
            whole = whole + share
        for h in range(PER):
            columns = pl.ds(h * TOK, TOK)
            mixed = jnp.zeros((HD, TOK), jnp.float32)
            for i in range(GROUP):
                mixed = mixed + parts[i, pl.ds(0, HD), columns].astype(jnp.float32) * (shares[i] / whole)[:, h * TOK:(h + 1) * TOK]
            attended[:, h * HD:(h + 1) * HD] = jnp.transpose(mixed).astype(jnp.bfloat16)

    out[...] = jnp.dot(attended[...], weight[...], preferred_element_type=jnp.float32).astype(jnp.bfloat16)


def project(parts, weight):
    width = weight.shape[1]
    step = 1024
    return pl.pallas_call(
        project_kernel,
        out_shape=jax.ShapeDtypeStruct((TOK, width), jnp.bfloat16),
        grid=(width // step,),
        in_specs=[
            pl.BlockSpec((GROUP, HD + STATS, ROWS), lambda n: (0, 0, 0)),
            pl.BlockSpec((ROWS, step), lambda n: (0, n)),
        ],
        out_specs=pl.BlockSpec((TOK, step), lambda n: (0, n)),
        scratch_shapes=[pltpu.VMEM((TOK, ROWS), jnp.bfloat16)],
        compiler_params=pltpu.CompilerParams(vmem_limit_bytes=16 << 20),
        name="project",
    )(parts, weight)


def spread(cache, queries):
    def shift(a, hops):
        pairs = [(y * NC + c, (y + hops * (1 - 2 * c)) % NY * NC + c) for y in range(NY) for c in range(NC)]
        return lax.ppermute(a, ("y", "c"), pairs)

    behind2, ahead2 = shift(cache, 2), shift(cache, -2)
    behind1, ahead1 = shift(cache, 1), shift(cache, -1)
    across, behind3, ahead3 = shift(behind2, 2), shift(behind2, 1), shift(ahead2, -1)
    same = lax.all_gather(queries, "x", axis=0)
    later = (behind1, ahead1, across, behind3, ahead3)
    same, behind1, ahead1, across, behind3, ahead3 = lax.optimization_barrier((same, *later))
    swapped = lax.ppermute(same, "c", [(0, 1), (1, 0)])
    return [cache, ahead1, ahead2, ahead3, across, behind3, behind2, behind1], [same, swapped]


def local(queries, new_kv, cache, block_owner, block_slot, prefix_blocks, out_weight):
    x, y, c = (lax.axis_index(name).reshape(1) for name in ("x", "y", "c"))
    shards, asked = spread(cache, queries)
    lists = block_lists(x, y, c, prefix_blocks, block_owner, block_slot)
    parts = attend(x, c, lists, new_kv, asked, shards)
    parts = lax.all_to_all(parts, ("x", "c"), split_axis=0, concat_axis=0, tiled=True)
    partial = project(parts, out_weight).reshape(NZ, TOK // NZ, -1)
    arrived = lax.all_to_all(partial, "z", split_axis=0, concat_axis=0, tiled=True)
    return jnp.sum(arrived.astype(jnp.float32), axis=0).astype(jnp.bfloat16)


def solution(mesh):
    fine = Mesh(mesh.devices.reshape(NX, NY, NC, NZ), ("x", "y", "c", "z"))
    replica = ("x", "y", "c")
    placed = (
        P(replica, "z"),
        P(None, replica, "z"),
        P(replica, None, None, "z"),
        P(),
        P(),
        P(),
        P("z", None),
    )
    return jax.shard_map(
        local, mesh=fine, in_specs=placed, out_specs=P(("x", "y", "c", "z"), None), check_vma=False
    )
```

time: 128 us -> 118 us (0.922)
  the two profiles are of different devices: /device:TPU:32 before, /device:TPU:16 now
where the time goes in v2:
time: 118 us
  blocking collectives  74.8 us (63%)
  starting transfers between devices  27.5 us (23%)
  Pallas kernels  9.97 us (8%)
  waiting for transfers between devices  3.81 us (3%)
    all_to_all x1, blocking collectives, local(): lax.all_to_all(partial, 'z', split_axis=0, concat_axis=0, tiled=True)  38.6 us
    ppermute x7, starting transfers between devices, shift(): return lax.ppermute(a, ('y', 'c'), pairs)  25.6 us
    all_to_all x1, blocking collectives, local(): lax.all_to_all(parts, ('x', 'c'), split_axis=0, concat_axis=0, tiled=True)  22.3 us
    all_gather x1, blocking collectives, spread(): same = lax.all_gather(queries, 'x', axis=0)  13.9 us
    pallas_call x1, Pallas kernels, attend(): pl.pallas_call(attend_kernel, out_shape=jax.ShapeDtypeStruct((GROUP, HD +...  6.98 us
    ppermute x7, waiting for transfers between devices, shift(): return lax.ppermute(a, ('y', 'c'), pairs)  3.6 us
  transfers between devices with their start and end apart: 8, of which 2 were waited for; matrix products, arithmetic and copies ran while one was open for 0% of the time, Pallas kernels for 1%

profile of v2, /device:TPU:16, one launch (start us, length us, event | category | flops | bytes accessed | tf_op | source)
XLA Modules:
  0.0 117.8 jit_solution(4919623443433235953)
XLA Ops:
  0.0 5.7 %collective-permute-start.2 = (bf16[8,2,64,128]{3,2,1,0:T(8,128)(2,1)}, bf16[8,2,64,128]{3,2,1,0:T(8,128)(2,1)S(1)}, u32[]{:S(2)}, u32[]{:S(2)}) collective-permute-start(bf16[8,2,64,128]{3,2,1,0:T(8,128)(2,1)} %rest_0_.1), channel_id=1, source_target_pairs={{0,32},{8,104},{16,48},{24,120},{32,64},{40,8},{48,80},{56,24},{64... | collective-permute-start | bytes 786440 | tf_op jit(solution)/shard_map/ppermute | solution.py:215
  5.7 3.8 %collective-permute-start.5 = (bf16[8,2,64,128]{3,2,1,0:T(8,128)(2,1)}, bf16[8,2,64,128]{3,2,1,0:T(8,128)(2,1)S(1)}, u32[]{:S(2)}, u32[]{:S(2)}) collective-permute-start(bf16[8,2,64,128]{3,2,1,0:T(8,128)(2,1)} %rest_0_.1), channel_id=1, source_target_pairs={{0,96},{8,40},{16,112},{24,56},{32,0},{40,72},{48,16},{56,88},{64,... | collective-permute-start | bytes 786440 | tf_op jit(solution)/shard_map/ppermute | solution.py:215
  9.5 1.9 %collective-permute-start.1 = (bf16[8,2,64,128]{3,2,1,0:T(8,128)(2,1)}, bf16[8,2,64,128]{3,2,1,0:T(8,128)(2,1)S(1)}, u32[]{:S(2)}, u32[]{:S(2)}) collective-permute-start(bf16[8,2,64,128]{3,2,1,0:T(8,128)(2,1)} %rest_0_.1), channel_id=1, source_target_pairs={{0,112},{8,24},{16,0},{24,40},{32,16},{40,56},{48,32},{56,72},{64,... | collective-permute-start | bytes 786440 | tf_op jit(solution)/shard_map/ppermute | solution.py:215
  11.5 3.9 %collective-permute-start = (bf16[8,2,64,128]{3,2,1,0:T(8,128)(2,1)}, bf16[8,2,64,128]{3,2,1,0:T(8,128)(2,1)S(1)}, u32[]{:S(2)}, u32[]{:S(2)}) collective-permute-start(bf16[8,2,64,128]{3,2,1,0:T(8,128)(2,1)} %rest_0_.1), channel_id=1, source_target_pairs={{0,16},{8,120},{16,32},{24,8},{32,48},{40,24},{48,64},{56,40},{64,... | collective-permute-start | bytes 786440 | tf_op jit(solution)/shard_map/ppermute | solution.py:215
  15.4 3.6 %collective-permute-done.2.rest_6_ = bf16[8,2,64,128]{3,2,1,0:T(8,128)(2,1)S(1)} collective-permute-done((bf16[8,2,64,128]{3,2,1,0:T(8,128)(2,1)}, bf16[8,2,64,128]{3,2,1,0:T(8,128)(2,1)S(1)}, u32[]{:S(2)}, u32[]{:S(2)}) %collective-permute-start.2) | collective-permute-done | bytes 262176 | tf_op jit(solution)/shard_map/ppermute | solution.py:215
  19.0 1.9 %collective-permute-start.4 = (bf16[8,2,64,128]{3,2,1,0:T(8,128)(2,1)S(1)}, bf16[8,2,64,128]{3,2,1,0:T(8,128)(2,1)S(1)}, u32[]{:S(2)}, u32[]{:S(2)}) collective-permute-start(bf16[8,2,64,128]{3,2,1,0:T(8,128)(2,1)S(1)} %collective-permute-done.2.rest_6_), channel_id=1, source_target_pairs={{0,16},{8,120},{16,32},{24,8},{32,48},{40,24},{48,64},{56,40},{64,... | collective-permute-start | bytes 786440 | tf_op jit(solution)/shard_map/ppermute | solution.py:215
  20.9 4.4 %collective-permute-start.3 = (bf16[8,2,64,128]{3,2,1,0:T(8,128)(2,1)S(1)}, bf16[8,2,64,128]{3,2,1,0:T(8,128)(2,1)S(1)}, u32[]{:S(2)}, u32[]{:S(2)}) collective-permute-start(bf16[8,2,64,128]{3,2,1,0:T(8,128)(2,1)S(1)} %collective-permute-done.2.rest_6_), channel_id=1, source_target_pairs={{0,32},{8,104},{16,48},{24,120},{32,64},{40,8},{48,80},{56,24},{64... | collective-permute-start | bytes 786440 | tf_op jit(solution)/shard_map/ppermute | solution.py:215
  25.3 0.0 collective-permute-done.5.rest_2_
  25.3 3.9 %collective-permute-start.6 = (bf16[8,2,64,128]{3,2,1,0:T(8,128)(2,1)S(1)}, bf16[8,2,64,128]{3,2,1,0:T(8,128)(2,1)S(1)}, u32[]{:S(2)}, u32[]{:S(2)}) collective-permute-start(bf16[8,2,64,128]{3,2,1,0:T(8,128)(2,1)S(1)} %collective-permute-done.5.rest_2_), channel_id=1, source_target_pairs={{0,112},{8,24},{16,0},{24,40},{32,16},{40,56},{48,32},{56,72},{64,... | collective-permute-start | bytes 786440 | tf_op jit(solution)/shard_map/ppermute | solution.py:215
  29.3 13.9 %all-gather = bf16[512,512]{1,0:T(8,128)(2,1)S(1)} all-gather(bf16[128,512]{1,0:T(8,128)(2,1)} %param.7), channel_id=2, replica_groups=mesh['x'=4,'y'=8,'c'=2,'z'=8] {'x'}, dimensions={0}, use_global_device_ids=true | all-gather | bytes 655360 | tf_op jit(solution)/shard_map/all_gather | solution.py:220
  43.2 0.0 collective-permute-done.1.rest_1_
  43.2 0.0 collective-permute-done.rest_7_
  43.2 0.0 collective-permute-done.4.rest_5_
  43.2 0.0 collective-permute-done.3.rest_4_
  43.2 0.0 collective-permute-done.6.rest_3_
  43.2 1.9 %collective-permute-start.7 = (bf16[4,128,512]{2,1,0:T(8,128)(2,1)S(1)}, bf16[4,128,512]{2,1,0:T(8,128)(2,1)S(1)}, u32[]{:S(2)}, u32[]{:S(2)}) collective-permute-start(bf16[4,128,512]{2,1,0:T(8,128)(2,1)S(1)} %bitcast.6), channel_id=1, source_target_pairs={{0,8},{8,0},{1,9},{9,1},{2,10},{10,2},{3,11},{11,3},{4,12},{12,4},... | collective-permute-start | bytes 1572872 | tf_op jit(solution)/shard_map/ppermute | solution.py:223
  45.2 0.0 copy-start.1
  45.2 0.6 copy-done.1
  45.8 1.0 block_lists.1.lists
  46.8 0.2 collective-permute-done.7.rest_9_
  47.0 0.0 copy-start
  47.0 7.0 %attend.1 = bf16[8,144,512]{2,1,0:T(8,128)(2,1)S(1)} custom-call(s32[1]{0:T(128)} %bitcast.x, s32[1]{0:T(128)} %bitcast.1.c, s32[8,128]{1,0:T(8,128)S(1)} %block_lists.1.lists, bf16[2,128,128]{2,1,0:T(8,128)(2,1)} %new_kv.1, bf16[8,2,64,128]{3,2,1,0:T(8,128)(2,1)} %rest_0_.1, bf16[8,2,64,128]{3,2,1,0:T(8,128)(2,1)S(1)} %collective-permute-done.1.rest_1_, ...), custom_call_target="tpu_custom_call" | custom-call | tf_op jit(solution)/shard_map/attend/pallas_call | solution.py:151
  54.0 22.3 %all_to_all.10.parts = bf16[8,144,512]{2,1,0:T(8,128)(2,1)S(1)} all-to-all(bf16[8,144,512]{2,1,0:T(8,128)(2,1)S(1)} %attend.1), channel_id=1, replica_groups=mesh['x'=4,'y'=8,'c'=2,'z'=8] {'x','c'}, dimensions={0} | all-to-all | bytes 2359296 | tf_op jit(solution)/shard_map/all_to_all | solution.py:232
  76.3 0.0 copy-done
  76.3 2.0 %project.1 = bf16[128,4096]{1,0:T(8,128)(2,1)S(1)} custom-call(bf16[8,144,512]{2,1,0:T(8,128)(2,1)S(1)} %all_to_all.10.parts, bf16[512,4096]{1,0:T(8,128)(2,1)S(1)} %copy-done), custom_call_target="tpu_custom_call" | custom-call | tf_op jit(solution)/shard_map/project/pallas_call | solution.py:197
  78.3 38.6 %all_to_all.11 = bf16[8,16,4096]{2,1,0:T(8,128)(2,1)S(1)} all-to-all(bf16[8,16,4096]{2,1,0:T(8,128)(2,1)S(1)} %bitcast.5), channel_id=1, replica_groups=mesh['x'=4,'y'=8,'c'=2,'z'=8] {'z'}, dimensions={0} | all-to-all | bytes 2097152 | tf_op jit(solution)/shard_map/all_to_all | solution.py:234
  116.9 0.8 reduce_sum.12
Async XLA Ops:
  0.0 19.0 %collective-permute-start.2 = (bf16[8,2,64,128]{3,2,1,0:T(8,128)(2,1)}, bf16[8,2,64,128]{3,2,1,0:T(8,128)(2,1)S(1)}, u32[]{:S(2)}, u32[]{:S(2)}) collective-permute-start(bf16[8,2,64,128]{3,2,1,0:T(8,128)(2,1)} %rest_0_.1), channel_id=1, source_target_pairs={{0,32},{8,104},{16,48},{24,120},{32,64},{40,8},{48,80},{56,24},{64... | collective-permute-start | bytes 786440 | tf_op jit(solution)/shard_map/ppermute | solution.py:215
  5.7 19.6 %collective-permute-start.5 = (bf16[8,2,64,128]{3,2,1,0:T(8,128)(2,1)}, bf16[8,2,64,128]{3,2,1,0:T(8,128)(2,1)S(1)}, u32[]{:S(2)}, u32[]{:S(2)}) collective-permute-start(bf16[8,2,64,128]{3,2,1,0:T(8,128)(2,1)} %rest_0_.1), channel_id=1, source_target_pairs={{0,96},{8,40},{16,112},{24,56},{32,0},{40,72},{48,16},{56,88},{64,... | collective-permute-start | bytes 786440 | tf_op jit(solution)/shard_map/ppermute | solution.py:215
  9.5 33.6 %collective-permute-start.1 = (bf16[8,2,64,128]{3,2,1,0:T(8,128)(2,1)}, bf16[8,2,64,128]{3,2,1,0:T(8,128)(2,1)S(1)}, u32[]{:S(2)}, u32[]{:S(2)}) collective-permute-start(bf16[8,2,64,128]{3,2,1,0:T(8,128)(2,1)} %rest_0_.1), channel_id=1, source_target_pairs={{0,112},{8,24},{16,0},{24,40},{32,16},{40,56},{48,32},{56,72},{64,... | collective-permute-start | bytes 786440 | tf_op jit(solution)/shard_map/ppermute | solution.py:215
  11.5 31.7 %collective-permute-start = (bf16[8,2,64,128]{3,2,1,0:T(8,128)(2,1)}, bf16[8,2,64,128]{3,2,1,0:T(8,128)(2,1)S(1)}, u32[]{:S(2)}, u32[]{:S(2)}) collective-permute-start(bf16[8,2,64,128]{3,2,1,0:T(8,128)(2,1)} %rest_0_.1), channel_id=1, source_target_pairs={{0,16},{8,120},{16,32},{24,8},{32,48},{40,24},{48,64},{56,40},{64,... | collective-permute-start | bytes 786440 | tf_op jit(solution)/shard_map/ppermute | solution.py:215
  19.0 24.2 %collective-permute-start.4 = (bf16[8,2,64,128]{3,2,1,0:T(8,128)(2,1)S(1)}, bf16[8,2,64,128]{3,2,1,0:T(8,128)(2,1)S(1)}, u32[]{:S(2)}, u32[]{:S(2)}) collective-permute-start(bf16[8,2,64,128]{3,2,1,0:T(8,128)(2,1)S(1)} %collective-permute-done.2.rest_6_), channel_id=1, source_target_pairs={{0,16},{8,120},{16,32},{24,8},{32,48},{40,24},{48,64},{56,40},{64,... | collective-permute-start | bytes 786440 | tf_op jit(solution)/shard_map/ppermute | solution.py:215
  20.9 22.3 %collective-permute-start.3 = (bf16[8,2,64,128]{3,2,1,0:T(8,128)(2,1)S(1)}, bf16[8,2,64,128]{3,2,1,0:T(8,128)(2,1)S(1)}, u32[]{:S(2)}, u32[]{:S(2)}) collective-permute-start(bf16[8,2,64,128]{3,2,1,0:T(8,128)(2,1)S(1)} %collective-permute-done.2.rest_6_), channel_id=1, source_target_pairs={{0,32},{8,104},{16,48},{24,120},{32,64},{40,8},{48,80},{56,24},{64... | collective-permute-start | bytes 786440 | tf_op jit(solution)/shard_map/ppermute | solution.py:215
  25.3 17.9 %collective-permute-start.6 = (bf16[8,2,64,128]{3,2,1,0:T(8,128)(2,1)S(1)}, bf16[8,2,64,128]{3,2,1,0:T(8,128)(2,1)S(1)}, u32[]{:S(2)}, u32[]{:S(2)}) collective-permute-start(bf16[8,2,64,128]{3,2,1,0:T(8,128)(2,1)S(1)} %collective-permute-done.5.rest_2_), channel_id=1, source_target_pairs={{0,112},{8,24},{16,0},{24,40},{32,16},{40,56},{48,32},{56,72},{64,... | collective-permute-start | bytes 786440 | tf_op jit(solution)/shard_map/ppermute | solution.py:215
  43.2 3.8 %collective-permute-start.7 = (bf16[4,128,512]{2,1,0:T(8,128)(2,1)S(1)}, bf16[4,128,512]{2,1,0:T(8,128)(2,1)S(1)}, u32[]{:S(2)}, u32[]{:S(2)}) collective-permute-start(bf16[4,128,512]{2,1,0:T(8,128)(2,1)S(1)} %bitcast.6), channel_id=1, source_target_pairs={{0,8},{8,0},{1,9},{9,1},{2,10},{10,2},{3,11},{11,3},{4,12},{12,4},... | collective-permute-start | bytes 1572872 | tf_op jit(solution)/shard_map/ppermute | solution.py:223
  45.2 0.7 copy-start.1
  47.0 29.3 %copy-start = (bf16[512,4096]{1,0:T(8,128)(2,1)S(1)}, bf16[512,4096]{1,0:T(8,128)(2,1)}, u32[]{:S(2)}) copy-start(bf16[512,4096]{1,0:T(8,128)(2,1)} %weight.1) | copy-start | bytes 12582916

commit v3 on v2

--- a/solution.py
+++ b/solution.py
@@ -21,7 +21,7 @@
 CAP = 2
 LIST = NY * CAP
 TILE = 4
-PAIR = 2
+PAIR = 4
 STATS = 16
 NEGATIVE = -1e30
 FLOOR = -1e29
@@ -66,7 +66,7 @@
 
 def attend_kernel(x, c, lists, new_kv, *rest):
     shards, asked, rest = rest[:NY], rest[NY:NY + NC], rest[NY + NC:]
-    out, queries, fresh, held, peak, total, weighted, sems = rest
+    out, queries, fresh, held, peak, total, weighted, order, sems = rest
     first = [pltpu.make_async_copy(asked[d], queries.at[d], sems.at[NY + d]) for d in range(NC)]
     first.append(pltpu.make_async_copy(new_kv, fresh, sems.at[NY + NC]))
     later = [pltpu.make_async_copy(shards[s], held.at[pl.ds(s * SLOTS, SLOTS)], sems.at[s]) for s in range(NY)]
@@ -78,71 +78,76 @@
         q = queries[(g + c[0]) % NC, g // NC]
         return jnp.concatenate([q[:, h * HD:(h + 1) * HD] for h in range(PER)], axis=0)
 
-    def fold(p, scores, values):
-        top = jnp.maximum(peak[p], jnp.max(scores, axis=0, keepdims=True))
-        factor = jnp.exp2((peak[p] - top) * LOG2)
+    def reduce(scores, values):
+        top = jnp.maximum(jnp.max(scores, axis=0, keepdims=True), FLOOR)
         weights = jnp.exp2((scores - top) * LOG2)
-        peak[p] = top
-        total[p] = total[p] * factor + jnp.sum(weights, axis=0, keepdims=True)
-        weighted[p] = weighted[p] * factor + contract(values, weights.astype(jnp.bfloat16), 0, 0)
-
-    def reset(p):
-        peak[p] = jnp.full((1, ROWS), FLOOR, jnp.float32)
-        total[p] = jnp.zeros((1, ROWS), jnp.float32)
-        weighted[p] = jnp.zeros((HD, ROWS), jnp.float32)
-
-    reset(0)
+        return top, jnp.sum(weights, axis=0, keepdims=True), contract(values, weights.astype(jnp.bfloat16), 0, 0)
+
+    def merge(g, top, amount, product):
+        highest = jnp.maximum(peak[g], top)
+        before, now = jnp.exp2((peak[g] - highest) * LOG2), jnp.exp2((top - highest) * LOG2)
+        peak[g] = highest
+        total[g] = total[g] * before + amount * now
+        weighted[g] = weighted[g] * before + product * now
+
+    def append(entry, used):
+        g, j = entry % GROUP, entry // GROUP
+        wanted = lists[g, LIST] > j * TILE
+
+        @pl.when(wanted)
+        def _():
+            order[used] = entry
+
+        return used + wanted.astype(jnp.int32)
+
+    peak[...] = jnp.full(peak.shape, FLOOR, jnp.float32)
+    total[...] = jnp.zeros(total.shape, jnp.float32)
+    weighted[...] = jnp.zeros(weighted.shape, jnp.float32)
+    used = lax.fori_loop(0, GROUP * LIST // TILE, append, 0)
+    for p in range(PAIR):
+        order[used + p] = GROUP * LIST // TILE
+
     for copy in first:
         copy.wait()
     scores = contract(fresh[0], heads(own), 1, 1)
     key = lax.broadcasted_iota(jnp.int32, (TOK, ROWS), 0)
     token = lax.broadcasted_iota(jnp.int32, (TOK, ROWS), 1) % TOK
-    fold(0, jnp.where(key <= token, scores, NEGATIVE), fresh[1])
+    merge(own, *reduce(jnp.where(key <= token, scores, NEGATIVE), fresh[1]))
     for copy in later:
         copy.wait()
 
-    def finish(p, g):
-        filled = total[p] > 0.0
-        safe = jnp.where(filled, total[p], 1.0)
-        level = jnp.where(filled, peak[p] * LOG2 + jnp.log2(safe), NEGATIVE)
+    def some_tiles(i, carry):
+        results = []
+        for p in range(PAIR):
+            entry = order[i * PAIR + p]
+            valid = entry < GROUP * LIST // TILE
+            g, j = entry % GROUP, jnp.where(valid, entry // GROUP, 0)
+            left = jnp.where(valid, (lists[g, LIST] - j * TILE) * BLOCK, 0)
+            ids = [lists[g, j * TILE + k] for k in range(TILE)]
+            keys = jnp.concatenate([held[b, 0] for b in ids], axis=0)
+            values = jnp.concatenate([held[b, 1] for b in ids], axis=0)
+            scores = contract(keys, heads(g), 1, 1)
+            place = lax.broadcasted_iota(jnp.int32, scores.shape, 0)
+            results.append((g, *reduce(jnp.where(place < left, scores, NEGATIVE), values)))
+        for result in results:
+            merge(*result)
+        return carry
+
+    lax.fori_loop(0, (used + PAIR - 1) // PAIR, some_tiles, 0)
+
+    def finish(g, carry):
+        filled = total[g] > 0.0
+        safe = jnp.where(filled, total[g], 1.0)
+        level = jnp.where(filled, peak[g] * LOG2 + jnp.log2(safe), NEGATIVE)
         high = level.astype(jnp.bfloat16).astype(jnp.float32)
         middle = (level - high).astype(jnp.bfloat16).astype(jnp.float32)
         row = lax.broadcasted_iota(jnp.int32, (STATS, ROWS), 0)
         stats = jnp.where(row == 0, high, jnp.where(row == 1, middle, jnp.where(row == 2, level - high - middle, 0.0)))
-        out[g, pl.ds(0, HD), :] = (weighted[p] * (1.0 / safe)).astype(jnp.bfloat16)
+        out[g, pl.ds(0, HD), :] = (weighted[g] * (1.0 / safe)).astype(jnp.bfloat16)
         out[g, pl.ds(HD, STATS), :] = stats.astype(jnp.bfloat16)
-
-    def one_pair(i, carry):
-        pair = [(own + i * PAIR + p) % GROUP for p in range(PAIR)]
-        counts = [lists[g, LIST] for g in pair]
-        for p in range(PAIR):
-            if p:
-                reset(p)
-            else:
-                pl.when(i > 0)(lambda: reset(0))
-
-        def one_tile(j, carry):
-            loaded = []
-            for g, count in zip(pair, counts):
-                ids = [lists[g, j * TILE + k] for k in range(TILE)]
-                keys = jnp.concatenate([held[b, 0] for b in ids], axis=0)
-                values = jnp.concatenate([held[b, 1] for b in ids], axis=0)
-                scores = contract(keys, heads(g), 1, 1)
-                place = lax.broadcasted_iota(jnp.int32, scores.shape, 0)
-                loaded.append((jnp.where(place < (count - j * TILE) * BLOCK, scores, NEGATIVE), values))
-            for p, (scores, values) in enumerate(loaded):
-                fold(p, scores, values)
-            return carry
-
-        longest = counts[0]
-        for count in counts[1:]:
-            longest = jnp.maximum(longest, count)
-        lax.fori_loop(0, (longest + TILE - 1) // TILE, one_tile, 0)
-        for p, g in enumerate(pair):
-            finish(p, g)
         return carry
 
-    lax.fori_loop(0, GROUP // PAIR, one_pair, 0)
+    lax.fori_loop(0, GROUP, finish, 0)
 
 
 def attend(x, c, lists, new_kv, asked, shards):
@@ -157,9 +162,10 @@
             pltpu.VMEM((NC, NX, TOK, ROWS), jnp.bfloat16),
             pltpu.VMEM((2, TOK, HD), jnp.bfloat16),
             pltpu.VMEM((NY * SLOTS, 2, BLOCK, HD), jnp.bfloat16),
-            pltpu.VMEM((PAIR, 1, ROWS), jnp.float32),
-            pltpu.VMEM((PAIR, 1, ROWS), jnp.float32),
-            pltpu.VMEM((PAIR, HD, ROWS), jnp.float32),
+            pltpu.VMEM((GROUP, 1, ROWS), jnp.float32),
+            pltpu.VMEM((GROUP, 1, ROWS), jnp.float32),
+            pltpu.VMEM((GROUP, HD, ROWS), jnp.float32),
+            pltpu.SMEM((GROUP * LIST // TILE + PAIR,), jnp.int32),
             pltpu.SemaphoreType.DMA((NY + NC + 1,)),
         ],
         compiler_params=pltpu.CompilerParams(vmem_limit_bytes=16 << 20),

time: 118 us -> 119 us (level)
  no operation moved by 1% of the time
where the time goes in v3:
time: 119 us; the launch traced here: 118 us
  blocking collectives  75 us (63%)
  starting transfers between devices  27.5 us (23%)
  Pallas kernels  10.3 us (9%)
  waiting for transfers between devices  3.81 us (3%)
    all_to_all x1, blocking collectives, local(): lax.all_to_all(partial, 'z', split_axis=0, concat_axis=0, tiled=True)  38.6 us
    ppermute x7, starting transfers between devices, shift(): return lax.ppermute(a, ('y', 'c'), pairs)  25.6 us
    all_to_all x1, blocking collectives, local(): lax.all_to_all(parts, ('x', 'c'), split_axis=0, concat_axis=0, tiled=True)  22.4 us
    all_gather x1, blocking collectives, spread(): same = lax.all_gather(queries, 'x', axis=0)  13.9 us
    pallas_call x1, Pallas kernels, attend(): pl.pallas_call(attend_kernel, out_shape=jax.ShapeDtypeStruct((GROUP, HD +...  7.35 us
    ppermute x7, waiting for transfers between devices, shift(): return lax.ppermute(a, ('y', 'c'), pairs)  3.6 us
  transfers between devices with their start and end apart: 8, of which 2 were waited for; matrix products, arithmetic and copies ran while one was open for 0% of the time, Pallas kernels for 1%

profile of v3, /device:TPU:16, one launch (start us, length us, event | category | flops | bytes accessed | tf_op | source)
XLA Modules:
  0.0 118.3 jit_solution(8994999791988480958)
XLA Ops:
  0.0 5.7 %collective-permute-start.2 = (bf16[8,2,64,128]{3,2,1,0:T(8,128)(2,1)}, bf16[8,2,64,128]{3,2,1,0:T(8,128)(2,1)S(1)}, u32[]{:S(2)}, u32[]{:S(2)}) collective-permute-start(bf16[8,2,64,128]{3,2,1,0:T(8,128)(2,1)} %rest_0_.1), channel_id=1, source_target_pairs={{0,32},{8,104},{16,48},{24,120},{32,64},{40,8},{48,80},{56,24},{64... | collective-permute-start | bytes 786440 | tf_op jit(solution)/shard_map/ppermute | solution.py:221
  5.7 3.8 %collective-permute-start.5 = (bf16[8,2,64,128]{3,2,1,0:T(8,128)(2,1)}, bf16[8,2,64,128]{3,2,1,0:T(8,128)(2,1)S(1)}, u32[]{:S(2)}, u32[]{:S(2)}) collective-permute-start(bf16[8,2,64,128]{3,2,1,0:T(8,128)(2,1)} %rest_0_.1), channel_id=1, source_target_pairs={{0,96},{8,40},{16,112},{24,56},{32,0},{40,72},{48,16},{56,88},{64,... | collective-permute-start | bytes 786440 | tf_op jit(solution)/shard_map/ppermute | solution.py:221
  9.5 1.9 %collective-permute-start.1 = (bf16[8,2,64,128]{3,2,1,0:T(8,128)(2,1)}, bf16[8,2,64,128]{3,2,1,0:T(8,128)(2,1)S(1)}, u32[]{:S(2)}, u32[]{:S(2)}) collective-permute-start(bf16[8,2,64,128]{3,2,1,0:T(8,128)(2,1)} %rest_0_.1), channel_id=1, source_target_pairs={{0,112},{8,24},{16,0},{24,40},{32,16},{40,56},{48,32},{56,72},{64,... | collective-permute-start | bytes 786440 | tf_op jit(solution)/shard_map/ppermute | solution.py:221
  11.5 3.9 %collective-permute-start = (bf16[8,2,64,128]{3,2,1,0:T(8,128)(2,1)}, bf16[8,2,64,128]{3,2,1,0:T(8,128)(2,1)S(1)}, u32[]{:S(2)}, u32[]{:S(2)}) collective-permute-start(bf16[8,2,64,128]{3,2,1,0:T(8,128)(2,1)} %rest_0_.1), channel_id=1, source_target_pairs={{0,16},{8,120},{16,32},{24,8},{32,48},{40,24},{48,64},{56,40},{64,... | collective-permute-start | bytes 786440 | tf_op jit(solution)/shard_map/ppermute | solution.py:221
  15.4 3.6 %collective-permute-done.2.rest_6_ = bf16[8,2,64,128]{3,2,1,0:T(8,128)(2,1)S(1)} collective-permute-done((bf16[8,2,64,128]{3,2,1,0:T(8,128)(2,1)}, bf16[8,2,64,128]{3,2,1,0:T(8,128)(2,1)S(1)}, u32[]{:S(2)}, u32[]{:S(2)}) %collective-permute-start.2) | collective-permute-done | bytes 262176 | tf_op jit(solution)/shard_map/ppermute | solution.py:221
  19.0 1.9 %collective-permute-start.4 = (bf16[8,2,64,128]{3,2,1,0:T(8,128)(2,1)S(1)}, bf16[8,2,64,128]{3,2,1,0:T(8,128)(2,1)S(1)}, u32[]{:S(2)}, u32[]{:S(2)}) collective-permute-start(bf16[8,2,64,128]{3,2,1,0:T(8,128)(2,1)S(1)} %collective-permute-done.2.rest_6_), channel_id=1, source_target_pairs={{0,16},{8,120},{16,32},{24,8},{32,48},{40,24},{48,64},{56,40},{64,... | collective-permute-start | bytes 786440 | tf_op jit(solution)/shard_map/ppermute | solution.py:221
  20.9 4.4 %collective-permute-start.3 = (bf16[8,2,64,128]{3,2,1,0:T(8,128)(2,1)S(1)}, bf16[8,2,64,128]{3,2,1,0:T(8,128)(2,1)S(1)}, u32[]{:S(2)}, u32[]{:S(2)}) collective-permute-start(bf16[8,2,64,128]{3,2,1,0:T(8,128)(2,1)S(1)} %collective-permute-done.2.rest_6_), channel_id=1, source_target_pairs={{0,32},{8,104},{16,48},{24,120},{32,64},{40,8},{48,80},{56,24},{64... | collective-permute-start | bytes 786440 | tf_op jit(solution)/shard_map/ppermute | solution.py:221
  25.3 0.0 collective-permute-done.5.rest_2_
  25.3 3.9 %collective-permute-start.6 = (bf16[8,2,64,128]{3,2,1,0:T(8,128)(2,1)S(1)}, bf16[8,2,64,128]{3,2,1,0:T(8,128)(2,1)S(1)}, u32[]{:S(2)}, u32[]{:S(2)}) collective-permute-start(bf16[8,2,64,128]{3,2,1,0:T(8,128)(2,1)S(1)} %collective-permute-done.5.rest_2_), channel_id=1, source_target_pairs={{0,112},{8,24},{16,0},{24,40},{32,16},{40,56},{48,32},{56,72},{64,... | collective-permute-start | bytes 786440 | tf_op jit(solution)/shard_map/ppermute | solution.py:221
  29.3 13.9 %all-gather = bf16[512,512]{1,0:T(8,128)(2,1)S(1)} all-gather(bf16[128,512]{1,0:T(8,128)(2,1)} %param.7), channel_id=2, replica_groups=mesh['x'=4,'y'=8,'c'=2,'z'=8] {'x'}, dimensions={0}, use_global_device_ids=true | all-gather | bytes 655360 | tf_op jit(solution)/shard_map/all_gather | solution.py:226
  43.2 0.0 collective-permute-done.1.rest_1_
  43.2 0.0 collective-permute-done.rest_7_
  43.2 0.0 collective-permute-done.4.rest_5_
  43.2 0.0 collective-permute-done.3.rest_4_
  43.2 0.0 collective-permute-done.6.rest_3_
  43.2 1.9 %collective-permute-start.7 = (bf16[4,128,512]{2,1,0:T(8,128)(2,1)S(1)}, bf16[4,128,512]{2,1,0:T(8,128)(2,1)S(1)}, u32[]{:S(2)}, u32[]{:S(2)}) collective-permute-start(bf16[4,128,512]{2,1,0:T(8,128)(2,1)S(1)} %bitcast.6), channel_id=1, source_target_pairs={{0,8},{8,0},{1,9},{9,1},{2,10},{10,2},{3,11},{11,3},{4,12},{12,4},... | collective-permute-start | bytes 1572872 | tf_op jit(solution)/shard_map/ppermute | solution.py:229
  45.2 0.0 copy-start.1
  45.2 0.6 copy-done.1
  45.8 1.0 block_lists.1.lists
  46.8 0.2 collective-permute-done.7.rest_9_
  47.0 0.0 copy-start
  47.0 7.3 %attend.1 = bf16[8,144,512]{2,1,0:T(8,128)(2,1)S(1)} custom-call(s32[1]{0:T(128)} %bitcast.x, s32[1]{0:T(128)} %bitcast.1.c, s32[8,128]{1,0:T(8,128)S(1)} %block_lists.1.lists, bf16[2,128,128]{2,1,0:T(8,128)(2,1)} %new_kv.1, bf16[8,2,64,128]{3,2,1,0:T(8,128)(2,1)} %rest_0_.1, bf16[8,2,64,128]{3,2,1,0:T(8,128)(2,1)S(1)} %collective-permute-done.1.rest_1_, ...), custom_call_target="tpu_custom_call" | custom-call | tf_op jit(solution)/shard_map/attend/pallas_call | solution.py:156
  54.4 22.4 %all_to_all.10.parts = bf16[8,144,512]{2,1,0:T(8,128)(2,1)S(1)} all-to-all(bf16[8,144,512]{2,1,0:T(8,128)(2,1)S(1)} %attend.1), channel_id=1, replica_groups=mesh['x'=4,'y'=8,'c'=2,'z'=8] {'x','c'}, dimensions={0} | all-to-all | bytes 2359296 | tf_op jit(solution)/shard_map/all_to_all | solution.py:238
  76.8 0.0 copy-done
  76.8 2.0 %project.1 = bf16[128,4096]{1,0:T(8,128)(2,1)S(1)} custom-call(bf16[8,144,512]{2,1,0:T(8,128)(2,1)S(1)} %all_to_all.10.parts, bf16[512,4096]{1,0:T(8,128)(2,1)S(1)} %copy-done), custom_call_target="tpu_custom_call" | custom-call | tf_op jit(solution)/shard_map/project/pallas_call | solution.py:203
  78.8 38.6 %all_to_all.11 = bf16[8,16,4096]{2,1,0:T(8,128)(2,1)S(1)} all-to-all(bf16[8,16,4096]{2,1,0:T(8,128)(2,1)S(1)} %bitcast.5), channel_id=1, replica_groups=mesh['x'=4,'y'=8,'c'=2,'z'=8] {'z'}, dimensions={0} | all-to-all | bytes 2097152 | tf_op jit(solution)/shard_map/all_to_all | solution.py:240
  117.5 0.8 reduce_sum.12
Async XLA Ops:
  0.0 19.0 %collective-permute-start.2 = (bf16[8,2,64,128]{3,2,1,0:T(8,128)(2,1)}, bf16[8,2,64,128]{3,2,1,0:T(8,128)(2,1)S(1)}, u32[]{:S(2)}, u32[]{:S(2)}) collective-permute-start(bf16[8,2,64,128]{3,2,1,0:T(8,128)(2,1)} %rest_0_.1), channel_id=1, source_target_pairs={{0,32},{8,104},{16,48},{24,120},{32,64},{40,8},{48,80},{56,24},{64... | collective-permute-start | bytes 786440 | tf_op jit(solution)/shard_map/ppermute | solution.py:221
  5.7 19.6 %collective-permute-start.5 = (bf16[8,2,64,128]{3,2,1,0:T(8,128)(2,1)}, bf16[8,2,64,128]{3,2,1,0:T(8,128)(2,1)S(1)}, u32[]{:S(2)}, u32[]{:S(2)}) collective-permute-start(bf16[8,2,64,128]{3,2,1,0:T(8,128)(2,1)} %rest_0_.1), channel_id=1, source_target_pairs={{0,96},{8,40},{16,112},{24,56},{32,0},{40,72},{48,16},{56,88},{64,... | collective-permute-start | bytes 786440 | tf_op jit(solution)/shard_map/ppermute | solution.py:221
  9.5 33.6 %collective-permute-start.1 = (bf16[8,2,64,128]{3,2,1,0:T(8,128)(2,1)}, bf16[8,2,64,128]{3,2,1,0:T(8,128)(2,1)S(1)}, u32[]{:S(2)}, u32[]{:S(2)}) collective-permute-start(bf16[8,2,64,128]{3,2,1,0:T(8,128)(2,1)} %rest_0_.1), channel_id=1, source_target_pairs={{0,112},{8,24},{16,0},{24,40},{32,16},{40,56},{48,32},{56,72},{64,... | collective-permute-start | bytes 786440 | tf_op jit(solution)/shard_map/ppermute | solution.py:221
  11.5 31.7 %collective-permute-start = (bf16[8,2,64,128]{3,2,1,0:T(8,128)(2,1)}, bf16[8,2,64,128]{3,2,1,0:T(8,128)(2,1)S(1)}, u32[]{:S(2)}, u32[]{:S(2)}) collective-permute-start(bf16[8,2,64,128]{3,2,1,0:T(8,128)(2,1)} %rest_0_.1), channel_id=1, source_target_pairs={{0,16},{8,120},{16,32},{24,8},{32,48},{40,24},{48,64},{56,40},{64,... | collective-permute-start | bytes 786440 | tf_op jit(solution)/shard_map/ppermute | solution.py:221
  19.0 24.2 %collective-permute-start.4 = (bf16[8,2,64,128]{3,2,1,0:T(8,128)(2,1)S(1)}, bf16[8,2,64,128]{3,2,1,0:T(8,128)(2,1)S(1)}, u32[]{:S(2)}, u32[]{:S(2)}) collective-permute-start(bf16[8,2,64,128]{3,2,1,0:T(8,128)(2,1)S(1)} %collective-permute-done.2.rest_6_), channel_id=1, source_target_pairs={{0,16},{8,120},{16,32},{24,8},{32,48},{40,24},{48,64},{56,40},{64,... | collective-permute-start | bytes 786440 | tf_op jit(solution)/shard_map/ppermute | solution.py:221
  20.9 22.3 %collective-permute-start.3 = (bf16[8,2,64,128]{3,2,1,0:T(8,128)(2,1)S(1)}, bf16[8,2,64,128]{3,2,1,0:T(8,128)(2,1)S(1)}, u32[]{:S(2)}, u32[]{:S(2)}) collective-permute-start(bf16[8,2,64,128]{3,2,1,0:T(8,128)(2,1)S(1)} %collective-permute-done.2.rest_6_), channel_id=1, source_target_pairs={{0,32},{8,104},{16,48},{24,120},{32,64},{40,8},{48,80},{56,24},{64... | collective-permute-start | bytes 786440 | tf_op jit(solution)/shard_map/ppermute | solution.py:221
  25.3 17.9 %collective-permute-start.6 = (bf16[8,2,64,128]{3,2,1,0:T(8,128)(2,1)S(1)}, bf16[8,2,64,128]{3,2,1,0:T(8,128)(2,1)S(1)}, u32[]{:S(2)}, u32[]{:S(2)}) collective-permute-start(bf16[8,2,64,128]{3,2,1,0:T(8,128)(2,1)S(1)} %collective-permute-done.5.rest_2_), channel_id=1, source_target_pairs={{0,112},{8,24},{16,0},{24,40},{32,16},{40,56},{48,32},{56,72},{64,... | collective-permute-start | bytes 786440 | tf_op jit(solution)/shard_map/ppermute | solution.py:221
  43.2 3.8 %collective-permute-start.7 = (bf16[4,128,512]{2,1,0:T(8,128)(2,1)S(1)}, bf16[4,128,512]{2,1,0:T(8,128)(2,1)S(1)}, u32[]{:S(2)}, u32[]{:S(2)}) collective-permute-start(bf16[4,128,512]{2,1,0:T(8,128)(2,1)S(1)} %bitcast.6), channel_id=1, source_target_pairs={{0,8},{8,0},{1,9},{9,1},{2,10},{10,2},{3,11},{11,3},{4,12},{12,4},... | collective-permute-start | bytes 1572872 | tf_op jit(solution)/shard_map/ppermute | solution.py:229
  45.2 0.7 copy-start.1
  47.0 29.8 %copy-start = (bf16[512,4096]{1,0:T(8,128)(2,1)S(1)}, bf16[512,4096]{1,0:T(8,128)(2,1)}, u32[]{:S(2)}) copy-start(bf16[512,4096]{1,0:T(8,128)(2,1)} %weight.1) | copy-start | bytes 12582916

commit v4 on v3

--- a/solution.py
+++ b/solution.py
@@ -1,3 +1,4 @@
+import functools
 import math
 
 import jax
@@ -21,6 +22,7 @@
 CAP = 2
 LIST = NY * CAP
 TILE = 4
+ENTRIES = NX * LIST // TILE
 PAIR = 4
 STATS = 16
 NEGATIVE = -1e30
@@ -64,18 +66,30 @@
     )(x, y, c, lengths, *(pltpu.with_memory_space_constraint(a, pltpu.HBM) for a in (owners, slots)))
 
 
-def attend_kernel(x, c, lists, new_kv, *rest):
-    shards, asked, rest = rest[:NY], rest[NY:NY + NC], rest[NY + NC:]
+def split_level(level):
+    high = level.astype(jnp.bfloat16).astype(jnp.float32)
+    middle = (level - high).astype(jnp.bfloat16).astype(jnp.float32)
+    row = lax.broadcasted_iota(jnp.int32, (STATS, ROWS), 0)
+    stats = jnp.where(row == 0, high, jnp.where(row == 1, middle, jnp.where(row == 2, level - high - middle, 0.0)))
+    return stats.astype(jnp.bfloat16)
+
+
+def join_level(stats):
+    stats = stats.astype(jnp.float32)
+    return stats[0:1] + stats[1:2] + stats[2:3]
+
+
+def attend_kernel(home, x, core, lists, new_kv, *rest):
+    shards, asked, rest = rest[:NY], rest[NY], rest[NY + 1:]
     out, queries, fresh, held, peak, total, weighted, order, sems = rest
-    first = [pltpu.make_async_copy(asked[d], queries.at[d], sems.at[NY + d]) for d in range(NC)]
-    first.append(pltpu.make_async_copy(new_kv, fresh, sems.at[NY + NC]))
+    first = [pltpu.make_async_copy(asked, queries, sems.at[NY])]
+    if home:
+        first.append(pltpu.make_async_copy(new_kv, fresh, sems.at[NY + 1]))
     later = [pltpu.make_async_copy(shards[s], held.at[pl.ds(s * SLOTS, SLOTS)], sems.at[s]) for s in range(NY)]
     for copy in first + later:
         copy.start()
-    own = x[0] * NC + c[0]
-
     def heads(g):
-        q = queries[(g + c[0]) % NC, g // NC]
+        q = queries[g]
         return jnp.concatenate([q[:, h * HD:(h + 1) * HD] for h in range(PER)], axis=0)
 
     def reduce(scores, values):
@@ -91,8 +105,8 @@
         weighted[g] = weighted[g] * before + product * now
 
     def append(entry, used):
-        g, j = entry % GROUP, entry // GROUP
-        wanted = lists[g, LIST] > j * TILE
+        g, j = entry % NX, entry // NX
+        wanted = lists[g * NC + core[0], LIST] > j * TILE
 
         @pl.when(wanted)
         def _():
@@ -103,16 +117,17 @@
     peak[...] = jnp.full(peak.shape, FLOOR, jnp.float32)
     total[...] = jnp.zeros(total.shape, jnp.float32)
     weighted[...] = jnp.zeros(weighted.shape, jnp.float32)
-    used = lax.fori_loop(0, GROUP * LIST // TILE, append, 0)
+    used = lax.fori_loop(0, ENTRIES, append, 0)
     for p in range(PAIR):
-        order[used + p] = GROUP * LIST // TILE
+        order[used + p] = ENTRIES
 
     for copy in first:
         copy.wait()
-    scores = contract(fresh[0], heads(own), 1, 1)
-    key = lax.broadcasted_iota(jnp.int32, (TOK, ROWS), 0)
-    token = lax.broadcasted_iota(jnp.int32, (TOK, ROWS), 1) % TOK
-    merge(own, *reduce(jnp.where(key <= token, scores, NEGATIVE), fresh[1]))
+    if home:
+        scores = contract(fresh[0], heads(x[0]), 1, 1)
+        key = lax.broadcasted_iota(jnp.int32, (TOK, ROWS), 0)
+        token = lax.broadcasted_iota(jnp.int32, (TOK, ROWS), 1) % TOK
+        merge(x[0], *reduce(jnp.where(key <= token, scores, NEGATIVE), fresh[1]))
     for copy in later:
         copy.wait()
 
@@ -120,10 +135,11 @@
         results = []
         for p in range(PAIR):
             entry = order[i * PAIR + p]
-            valid = entry < GROUP * LIST // TILE
-            g, j = entry % GROUP, jnp.where(valid, entry // GROUP, 0)
-            left = jnp.where(valid, (lists[g, LIST] - j * TILE) * BLOCK, 0)
-            ids = [lists[g, j * TILE + k] for k in range(TILE)]
+            valid = entry < ENTRIES
+            g, j = entry % NX, jnp.where(valid, entry // NX, 0)
+            row = g * NC + core[0]
+            left = jnp.where(valid, (lists[row, LIST] - j * TILE) * BLOCK, 0)
+            ids = [lists[row, j * TILE + k] for k in range(TILE)]
             keys = jnp.concatenate([held[b, 0] for b in ids], axis=0)
             values = jnp.concatenate([held[b, 1] for b in ids], axis=0)
             scores = contract(keys, heads(g), 1, 1)
@@ -139,47 +155,66 @@
         filled = total[g] > 0.0
         safe = jnp.where(filled, total[g], 1.0)
         level = jnp.where(filled, peak[g] * LOG2 + jnp.log2(safe), NEGATIVE)
-        high = level.astype(jnp.bfloat16).astype(jnp.float32)
-        middle = (level - high).astype(jnp.bfloat16).astype(jnp.float32)
-        row = lax.broadcasted_iota(jnp.int32, (STATS, ROWS), 0)
-        stats = jnp.where(row == 0, high, jnp.where(row == 1, middle, jnp.where(row == 2, level - high - middle, 0.0)))
         out[g, pl.ds(0, HD), :] = (weighted[g] * (1.0 / safe)).astype(jnp.bfloat16)
-        out[g, pl.ds(HD, STATS), :] = stats.astype(jnp.bfloat16)
+        out[g, pl.ds(HD, STATS), :] = split_level(level)
         return carry
 
-    lax.fori_loop(0, GROUP, finish, 0)
-
-
-def attend(x, c, lists, new_kv, asked, shards):
+    lax.fori_loop(0, NX, finish, 0)
+
+
+def attend(home, x, core, lists, new_kv, asked, shards):
     vmem, smem, free = (pl.BlockSpec(memory_space=m) for m in (pltpu.VMEM, pltpu.SMEM, pl.ANY))
     new_kv, own = (pltpu.with_memory_space_constraint(a, pltpu.HBM) for a in (new_kv, shards[0]))
     return pl.pallas_call(
-        attend_kernel,
-        out_shape=jax.ShapeDtypeStruct((GROUP, HD + STATS, ROWS), jnp.bfloat16),
-        in_specs=[smem, smem, smem] + [free] * (1 + NC + NY),
+        functools.partial(attend_kernel, home),
+        out_shape=jax.ShapeDtypeStruct((NX, HD + STATS, ROWS), jnp.bfloat16),
+        in_specs=[smem, smem, smem] + [free] * (2 + NY),
         out_specs=vmem,
         scratch_shapes=[
-            pltpu.VMEM((NC, NX, TOK, ROWS), jnp.bfloat16),
+            pltpu.VMEM((NX, TOK, ROWS), jnp.bfloat16),
             pltpu.VMEM((2, TOK, HD), jnp.bfloat16),
             pltpu.VMEM((NY * SLOTS, 2, BLOCK, HD), jnp.bfloat16),
-            pltpu.VMEM((GROUP, 1, ROWS), jnp.float32),
-            pltpu.VMEM((GROUP, 1, ROWS), jnp.float32),
-            pltpu.VMEM((GROUP, HD, ROWS), jnp.float32),
-            pltpu.SMEM((GROUP * LIST // TILE + PAIR,), jnp.int32),
-            pltpu.SemaphoreType.DMA((NY + NC + 1,)),
+            pltpu.VMEM((NX, 1, ROWS), jnp.float32),
+            pltpu.VMEM((NX, 1, ROWS), jnp.float32),
+            pltpu.VMEM((NX, HD, ROWS), jnp.float32),
+            pltpu.SMEM((ENTRIES + PAIR,), jnp.int32),
+            pltpu.SemaphoreType.DMA((NY + 2,)),
         ],
         compiler_params=pltpu.CompilerParams(vmem_limit_bytes=16 << 20),
-        name="attend",
-    )(x, c, lists, new_kv, own, *shards[1:], *asked)
+        name="attend_home" if home else "attend_other",
+    )(x, core, lists, new_kv, own, *shards[1:], asked)
+
+
+def combine_kernel(one, two, out):
+    for g in range(NX):
+        levels = [join_level(part[g, pl.ds(HD, STATS), :]) for part in (one, two)]
+        top = jnp.maximum(*levels)
+        shares = [jnp.exp2(level - top) for level in levels]
+        whole = shares[0] + shares[1]
+        inverse = 1.0 / whole
+        rows = [part[g, pl.ds(0, HD), :].astype(jnp.float32) * (share * inverse) for part, share in zip((one, two), shares)]
+        out[g, pl.ds(0, HD), :] = (rows[0] + rows[1]).astype(jnp.bfloat16)
+        out[g, pl.ds(HD, STATS), :] = split_level(top + jnp.log2(whole))
+
+
+def combine(one, two):
+    vmem = pl.BlockSpec(memory_space=pltpu.VMEM)
+    return pl.pallas_call(
+        combine_kernel,
+        out_shape=jax.ShapeDtypeStruct(one.shape, one.dtype),
+        in_specs=[vmem, vmem],
+        out_specs=vmem,
+        compiler_params=pltpu.CompilerParams(vmem_limit_bytes=8 << 20),
+        name="combine",
+    )(one, two)
 
 
 def project_kernel(parts, weight, out, attended):
     @pl.when(pl.program_id(0) == 0)
     def _():
         levels = []
-        for i in range(GROUP):
-            stats = parts[i, pl.ds(HD, STATS), :].astype(jnp.float32)
-            levels.append(stats[0:1] + stats[1:2] + stats[2:3])
+        for i in range(NX):
+            levels.append(join_level(parts[i, pl.ds(HD, STATS), :]))
         top = levels[0]
         for level in levels[1:]:
             top = jnp.maximum(top, level)
@@ -190,7 +225,7 @@
         for h in range(PER):
             columns = pl.ds(h * TOK, TOK)
             mixed = jnp.zeros((HD, TOK), jnp.float32)
-            for i in range(GROUP):
+            for i in range(NX):
                 mixed = mixed + parts[i, pl.ds(0, HD), columns].astype(jnp.float32) * (shares[i] / whole)[:, h * TOK:(h + 1) * TOK]
             attended[:, h * HD:(h + 1) * HD] = jnp.transpose(mixed).astype(jnp.bfloat16)
 
@@ -205,7 +240,7 @@
         out_shape=jax.ShapeDtypeStruct((TOK, width), jnp.bfloat16),
         grid=(width // step,),
         in_specs=[
-            pl.BlockSpec((GROUP, HD + STATS, ROWS), lambda n: (0, 0, 0)),
+            pl.BlockSpec((NX, HD + STATS, ROWS), lambda n: (0, 0, 0)),
             pl.BlockSpec((ROWS, step), lambda n: (0, n)),
         ],
         out_specs=pl.BlockSpec((TOK, step), lambda n: (0, n)),
@@ -234,8 +269,11 @@
     x, y, c = (lax.axis_index(name).reshape(1) for name in ("x", "y", "c"))
     shards, asked = spread(cache, queries)
     lists = block_lists(x, y, c, prefix_blocks, block_owner, block_slot)
-    parts = attend(x, c, lists, new_kv, asked, shards)
-    parts = lax.all_to_all(parts, ("x", "c"), split_axis=0, concat_axis=0, tiled=True)
+    other = attend(False, x, 1 - c, lists, new_kv, asked[1], shards)
+    lists, other = lax.optimization_barrier((lists, other))
+    returned = lax.ppermute(other, "c", [(0, 1), (1, 0)])
+    parts = combine(attend(True, x, c, lists, new_kv, asked[0], shards), returned)
+    parts = lax.all_to_all(parts, "x", split_axis=0, concat_axis=0, tiled=True)
     partial = project(parts, out_weight).reshape(NZ, TOK // NZ, -1)
     arrived = lax.all_to_all(partial, "z", split_axis=0, concat_axis=0, tiled=True)
     return jnp.sum(arrived.astype(jnp.float32), axis=0).astype(jnp.bfloat16)

time: 119 us -> 115 us (0.966)
  the two profiles are of different devices: /device:TPU:16 before, /device:TPU:1 now
where the time goes in v4:
time: 115 us; the launch traced here: 114 us
  blocking collectives  65.6 us (57%)
  starting transfers between devices  33.1 us (29%)
  Pallas kernels  10.6 us (9%)
  waiting for transfers between devices  3.47 us (3%)
    all_to_all x1, blocking collectives, local(): lax.all_to_all(partial, 'z', split_axis=0, concat_axis=0, tiled=True)  39 us
    ppermute x7, starting transfers between devices, shift(): return lax.ppermute(a, ('y', 'c'), pairs)  24.5 us
    all_to_all x1, blocking collectives, local(): parts = lax.all_to_all(parts, 'x', split_axis=0, concat_axis=0, tiled=True)  14.9 us
    all_gather x1, blocking collectives, spread(): same = lax.all_gather(queries, 'x', axis=0)  11.8 us
    pallas_call x2, Pallas kernels, attend(): pl.pallas_call(functools.partial(attend_kernel, home), out_shape=jax.Shap...  7.44 us
    ppermute x1, starting transfers between devices, spread(): swapped = lax.ppermute(same, 'c', [(0, 1), (1, 0)])  4.96 us
    ppermute x1, starting transfers between devices, local(): returned = lax.ppermute(other, 'c', [(0, 1), (1, 0)])  3.69 us
    ppermute x7, waiting for transfers between devices, shift(): return lax.ppermute(a, ('y', 'c'), pairs)  3.46 us
  transfers between devices with their start and end apart: 9, of which 1 were waited for; matrix products, arithmetic and copies ran while one was open for 0% of the time, Pallas kernels for 4%

profile of v4, /device:TPU:1, one launch (start us, length us, event | category | flops | bytes accessed | tf_op | source)
XLA Modules:
  0.0 114.5 jit_solution(7724970293197792533)
XLA Ops:
  0.0 5.0 %collective-permute-start.5 = (bf16[8,2,64,128]{3,2,1,0:T(8,128)(2,1)}, bf16[8,2,64,128]{3,2,1,0:T(8,128)(2,1)S(1)}, u32[]{:S(2)}, u32[]{:S(2)}) collective-permute-start(bf16[8,2,64,128]{3,2,1,0:T(8,128)(2,1)} %rest_0_.3), channel_id=1, source_target_pairs={{0,96},{8,40},{16,112},{24,56},{32,0},{40,72},{48,16},{56,88},{64,... | collective-permute-start | bytes 786440 | tf_op jit(solution)/shard_map/ppermute | solution.py:256
  5.0 3.6 %collective-permute-start.2 = (bf16[8,2,64,128]{3,2,1,0:T(8,128)(2,1)}, bf16[8,2,64,128]{3,2,1,0:T(8,128)(2,1)S(1)}, u32[]{:S(2)}, u32[]{:S(2)}) collective-permute-start(bf16[8,2,64,128]{3,2,1,0:T(8,128)(2,1)} %rest_0_.3), channel_id=1, source_target_pairs={{0,32},{8,104},{16,48},{24,120},{32,64},{40,8},{48,80},{56,24},{64... | collective-permute-start | bytes 786440 | tf_op jit(solution)/shard_map/ppermute | solution.py:256
  8.6 2.8 %collective-permute-start.1 = (bf16[8,2,64,128]{3,2,1,0:T(8,128)(2,1)}, bf16[8,2,64,128]{3,2,1,0:T(8,128)(2,1)S(1)}, u32[]{:S(2)}, u32[]{:S(2)}) collective-permute-start(bf16[8,2,64,128]{3,2,1,0:T(8,128)(2,1)} %rest_0_.3), channel_id=1, source_target_pairs={{0,112},{8,24},{16,0},{24,40},{32,16},{40,56},{48,32},{56,72},{64,... | collective-permute-start | bytes 786440 | tf_op jit(solution)/shard_map/ppermute | solution.py:256
  11.4 3.7 %collective-permute-start = (bf16[8,2,64,128]{3,2,1,0:T(8,128)(2,1)}, bf16[8,2,64,128]{3,2,1,0:T(8,128)(2,1)S(1)}, u32[]{:S(2)}, u32[]{:S(2)}) collective-permute-start(bf16[8,2,64,128]{3,2,1,0:T(8,128)(2,1)} %rest_0_.3), channel_id=1, source_target_pairs={{0,16},{8,120},{16,32},{24,8},{32,48},{40,24},{48,64},{56,40},{64,... | collective-permute-start | bytes 786440 | tf_op jit(solution)/shard_map/ppermute | solution.py:256
  15.2 0.0 collective-permute-done.5.rest_2_
  15.2 1.9 %collective-permute-start.6 = (bf16[8,2,64,128]{3,2,1,0:T(8,128)(2,1)S(1)}, bf16[8,2,64,128]{3,2,1,0:T(8,128)(2,1)S(1)}, u32[]{:S(2)}, u32[]{:S(2)}) collective-permute-start(bf16[8,2,64,128]{3,2,1,0:T(8,128)(2,1)S(1)} %collective-permute-done.5.rest_2_), channel_id=1, source_target_pairs={{0,112},{8,24},{16,0},{24,40},{32,16},{40,56},{48,32},{56,72},{64,... | collective-permute-start | bytes 786440 | tf_op jit(solution)/shard_map/ppermute | solution.py:256
  17.1 3.4 %collective-permute-done.2.rest_6_ = bf16[8,2,64,128]{3,2,1,0:T(8,128)(2,1)S(1)} collective-permute-done((bf16[8,2,64,128]{3,2,1,0:T(8,128)(2,1)}, bf16[8,2,64,128]{3,2,1,0:T(8,128)(2,1)S(1)}, u32[]{:S(2)}, u32[]{:S(2)}) %collective-permute-start.2) | collective-permute-done | bytes 262176 | tf_op jit(solution)/shard_map/ppermute | solution.py:256
  20.5 4.2 %collective-permute-start.4 = (bf16[8,2,64,128]{3,2,1,0:T(8,128)(2,1)S(1)}, bf16[8,2,64,128]{3,2,1,0:T(8,128)(2,1)S(1)}, u32[]{:S(2)}, u32[]{:S(2)}) collective-permute-start(bf16[8,2,64,128]{3,2,1,0:T(8,128)(2,1)S(1)} %collective-permute-done.2.rest_6_), channel_id=1, source_target_pairs={{0,16},{8,120},{16,32},{24,8},{32,48},{40,24},{48,64},{56,40},{64,... | collective-permute-start | bytes 786440 | tf_op jit(solution)/shard_map/ppermute | solution.py:256
  24.7 3.3 %collective-permute-start.3 = (bf16[8,2,64,128]{3,2,1,0:T(8,128)(2,1)S(1)}, bf16[8,2,64,128]{3,2,1,0:T(8,128)(2,1)S(1)}, u32[]{:S(2)}, u32[]{:S(2)}) collective-permute-start(bf16[8,2,64,128]{3,2,1,0:T(8,128)(2,1)S(1)} %collective-permute-done.2.rest_6_), channel_id=1, source_target_pairs={{0,32},{8,104},{16,48},{24,120},{32,64},{40,8},{48,80},{56,24},{64... | collective-permute-start | bytes 786440 | tf_op jit(solution)/shard_map/ppermute | solution.py:256
  28.0 11.8 %all-gather = bf16[512,512]{1,0:T(8,128)(2,1)S(1)} all-gather(bf16[128,512]{1,0:T(8,128)(2,1)} %param.7), channel_id=2, replica_groups=mesh['x'=4,'y'=8,'c'=2,'z'=8] {'x'}, dimensions={0}, use_global_device_ids=true | all-gather | bytes 655360 | tf_op jit(solution)/shard_map/all_gather | solution.py:261
  39.8 0.0 collective-permute-done.1.rest_1_
  39.8 0.0 collective-permute-done.rest_7_
  39.8 0.0 collective-permute-done.6.rest_3_
  39.8 0.0 collective-permute-done.4.rest_5_
  39.8 0.0 collective-permute-done.3.rest_4_
  39.8 5.0 %collective-permute-start.7 = (bf16[4,128,512]{2,1,0:T(8,128)(2,1)S(1)}, bf16[4,128,512]{2,1,0:T(8,128)(2,1)S(1)}, u32[]{:S(2)}, u32[]{:S(2)}) collective-permute-start(bf16[4,128,512]{2,1,0:T(8,128)(2,1)S(1)} %bitcast.6), channel_id=1, source_target_pairs={{0,8},{8,0},{1,9},{9,1},{2,10},{10,2},{3,11},{11,3},{4,12},{12,4},... | collective-permute-start | bytes 1572872 | tf_op jit(solution)/shard_map/ppermute | solution.py:264
  44.8 0.0 copy-start.1
  44.8 0.6 copy-done.1
  45.4 1.0 block_lists.1.lists
  46.5 0.0 copy-start
  46.5 0.0 collective-permute-done.7.rest_8_
  46.5 3.7 %attend_other.1 = bf16[4,144,512]{2,1,0:T(8,128)(2,1)S(1)} custom-call(s32[1]{0:T(128)} %bitcast.x, s32[1]{0:T(128)S(6)} %sub.3.core, s32[8,128]{1,0:T(8,128)S(1)} %block_lists.1.lists, bf16[2,128,128]{2,1,0:T(8,128)(2,1)} %new_kv.3, bf16[8,2,64,128]{3,2,1,0:T(8,128)(2,1)} %rest_0_.3, bf16[8,2,64,128]{3,2,1,0:T(8,128)(2,1)S(1)} %collective-permute-done.1.rest_1_, ...), custom_call_target="tpu_custom_call" | custom-call | tf_op jit(solution)/shard_map/attend_other/pallas_call | solution.py:168
  50.2 3.7 %collective-permute-start.8 = (bf16[4,144,512]{2,1,0:T(8,128)(2,1)S(1)}, bf16[4,144,512]{2,1,0:T(8,128)(2,1)S(1)}, u32[]{:S(2)}, u32[]{:S(2)}) collective-permute-start(bf16[4,144,512]{2,1,0:T(8,128)(2,1)S(1)} %attend_other.1), channel_id=1, source_target_pairs={{0,8},{8,0},{1,9},{9,1},{2,10},{10,2},{3,11},{11,3},{4,12},{12,4},... | collective-permute-start | bytes 1769480 | tf_op jit(solution)/shard_map/ppermute | solution.py:274
  53.9 3.7 %attend_home.1.one = bf16[4,144,512]{2,1,0:T(8,128)(2,1)S(1)} custom-call(s32[1]{0:T(128)} %bitcast.x, s32[1]{0:T(128)} %bitcast.1.c.core, s32[8,128]{1,0:T(8,128)S(1)} %block_lists.1.lists, bf16[2,128,128]{2,1,0:T(8,128)(2,1)} %new_kv.3, bf16[8,2,64,128]{3,2,1,0:T(8,128)(2,1)} %rest_0_.3, bf16[8,2,64,128]{3,2,1,0:T(8,128)(2,1)S(1)} %collective-permute-done.1.rest_1_, ...), custom_call_target="tpu_custom_call" | custom-call | tf_op jit(solution)/shard_map/attend_home/pallas_call | solution.py:168
  57.6 0.0 collective-permute-done.8.two
  57.6 0.3 combine.1
  57.9 14.9 %all_to_all.10.parts = bf16[4,144,512]{2,1,0:T(8,128)(2,1)S(1)} all-to-all(bf16[4,144,512]{2,1,0:T(8,128)(2,1)S(1)} %combine.1), channel_id=1, replica_groups=mesh['x'=4,'y'=8,'c'=2,'z'=8] {'x'}, dimensions={0} | all-to-all | bytes 1179648 | tf_op jit(solution)/shard_map/all_to_all | solution.py:276
  72.8 0.0 copy-done
  72.8 1.8 %project.1 = bf16[128,4096]{1,0:T(8,128)(2,1)S(1)} custom-call(bf16[4,144,512]{2,1,0:T(8,128)(2,1)S(1)} %all_to_all.10.parts, bf16[512,4096]{1,0:T(8,128)(2,1)S(1)} %copy-done), custom_call_target="tpu_custom_call" | custom-call | tf_op jit(solution)/shard_map/project/pallas_call | solution.py:238
  74.6 39.0 %all_to_all.11 = bf16[8,16,4096]{2,1,0:T(8,128)(2,1)S(1)} all-to-all(bf16[8,16,4096]{2,1,0:T(8,128)(2,1)S(1)} %bitcast.5), channel_id=1, replica_groups=mesh['x'=4,'y'=8,'c'=2,'z'=8] {'z'}, dimensions={0} | all-to-all | bytes 2097152 | tf_op jit(solution)/shard_map/all_to_all | solution.py:278
  113.6 0.8 reduce_sum.12
Async XLA Ops:
  0.0 15.2 %collective-permute-start.5 = (bf16[8,2,64,128]{3,2,1,0:T(8,128)(2,1)}, bf16[8,2,64,128]{3,2,1,0:T(8,128)(2,1)S(1)}, u32[]{:S(2)}, u32[]{:S(2)}) collective-permute-start(bf16[8,2,64,128]{3,2,1,0:T(8,128)(2,1)} %rest_0_.3), channel_id=1, source_target_pairs={{0,96},{8,40},{16,112},{24,56},{32,0},{40,72},{48,16},{56,88},{64,... | collective-permute-start | bytes 786440 | tf_op jit(solution)/shard_map/ppermute | solution.py:256
  5.0 15.5 %collective-permute-start.2 = (bf16[8,2,64,128]{3,2,1,0:T(8,128)(2,1)}, bf16[8,2,64,128]{3,2,1,0:T(8,128)(2,1)S(1)}, u32[]{:S(2)}, u32[]{:S(2)}) collective-permute-start(bf16[8,2,64,128]{3,2,1,0:T(8,128)(2,1)} %rest_0_.3), channel_id=1, source_target_pairs={{0,32},{8,104},{16,48},{24,120},{32,64},{40,8},{48,80},{56,24},{64... | collective-permute-start | bytes 786440 | tf_op jit(solution)/shard_map/ppermute | solution.py:256
  8.6 31.1 %collective-permute-start.1 = (bf16[8,2,64,128]{3,2,1,0:T(8,128)(2,1)}, bf16[8,2,64,128]{3,2,1,0:T(8,128)(2,1)S(1)}, u32[]{:S(2)}, u32[]{:S(2)}) collective-permute-start(bf16[8,2,64,128]{3,2,1,0:T(8,128)(2,1)} %rest_0_.3), channel_id=1, source_target_pairs={{0,112},{8,24},{16,0},{24,40},{32,16},{40,56},{48,32},{56,72},{64,... | collective-permute-start | bytes 786440 | tf_op jit(solution)/shard_map/ppermute | solution.py:256
  11.4 28.3 %collective-permute-start = (bf16[8,2,64,128]{3,2,1,0:T(8,128)(2,1)}, bf16[8,2,64,128]{3,2,1,0:T(8,128)(2,1)S(1)}, u32[]{:S(2)}, u32[]{:S(2)}) collective-permute-start(bf16[8,2,64,128]{3,2,1,0:T(8,128)(2,1)} %rest_0_.3), channel_id=1, source_target_pairs={{0,16},{8,120},{16,32},{24,8},{32,48},{40,24},{48,64},{56,40},{64,... | collective-permute-start | bytes 786440 | tf_op jit(solution)/shard_map/ppermute | solution.py:256
  15.2 24.6 %collective-permute-start.6 = (bf16[8,2,64,128]{3,2,1,0:T(8,128)(2,1)S(1)}, bf16[8,2,64,128]{3,2,1,0:T(8,128)(2,1)S(1)}, u32[]{:S(2)}, u32[]{:S(2)}) collective-permute-start(bf16[8,2,64,128]{3,2,1,0:T(8,128)(2,1)S(1)} %collective-permute-done.5.rest_2_), channel_id=1, source_target_pairs={{0,112},{8,24},{16,0},{24,40},{32,16},{40,56},{48,32},{56,72},{64,... | collective-permute-start | bytes 786440 | tf_op jit(solution)/shard_map/ppermute | solution.py:256
  20.5 19.3 %collective-permute-start.4 = (bf16[8,2,64,128]{3,2,1,0:T(8,128)(2,1)S(1)}, bf16[8,2,64,128]{3,2,1,0:T(8,128)(2,1)S(1)}, u32[]{:S(2)}, u32[]{:S(2)}) collective-permute-start(bf16[8,2,64,128]{3,2,1,0:T(8,128)(2,1)S(1)} %collective-permute-done.2.rest_6_), channel_id=1, source_target_pairs={{0,16},{8,120},{16,32},{24,8},{32,48},{40,24},{48,64},{56,40},{64,... | collective-permute-start | bytes 786440 | tf_op jit(solution)/shard_map/ppermute | solution.py:256
  24.7 15.1 %collective-permute-start.3 = (bf16[8,2,64,128]{3,2,1,0:T(8,128)(2,1)S(1)}, bf16[8,2,64,128]{3,2,1,0:T(8,128)(2,1)S(1)}, u32[]{:S(2)}, u32[]{:S(2)}) collective-permute-start(bf16[8,2,64,128]{3,2,1,0:T(8,128)(2,1)S(1)} %collective-permute-done.2.rest_6_), channel_id=1, source_target_pairs={{0,32},{8,104},{16,48},{24,120},{32,64},{40,8},{48,80},{56,24},{64... | collective-permute-start | bytes 786440 | tf_op jit(solution)/shard_map/ppermute | solution.py:256
  39.8 6.7 %collective-permute-start.7 = (bf16[4,128,512]{2,1,0:T(8,128)(2,1)S(1)}, bf16[4,128,512]{2,1,0:T(8,128)(2,1)S(1)}, u32[]{:S(2)}, u32[]{:S(2)}) collective-permute-start(bf16[4,128,512]{2,1,0:T(8,128)(2,1)S(1)} %bitcast.6), channel_id=1, source_target_pairs={{0,8},{8,0},{1,9},{9,1},{2,10},{10,2},{3,11},{11,3},{4,12},{12,4},... | collective-permute-start | bytes 1572872 | tf_op jit(solution)/shard_map/ppermute | solution.py:264
  44.8 0.7 copy-start.1
  46.5 26.3 %copy-start = (bf16[512,4096]{1,0:T(8,128)(2,1)S(1)}, bf16[512,4096]{1,0:T(8,128)(2,1)}, u32[]{:S(2)}) copy-start(bf16[512,4096]{1,0:T(8,128)(2,1)} %weight.1) | copy-start | bytes 12582916
  50.2 7.4 %collective-permute-start.8 = (bf16[4,144,512]{2,1,0:T(8,128)(2,1)S(1)}, bf16[4,144,512]{2,1,0:T(8,128)(2,1)S(1)}, u32[]{:S(2)}, u32[]{:S(2)}) collective-permute-start(bf16[4,144,512]{2,1,0:T(8,128)(2,1)S(1)} %attend_other.1), channel_id=1, source_target_pairs={{0,8},{8,0},{1,9},{9,1},{2,10},{10,2},{3,11},{11,3},{4,12},{12,4},... | collective-permute-start | bytes 1769480 | tf_op jit(solution)/shard_map/ppermute | solution.py:274

commit v5 on v4

--- a/solution.py
+++ b/solution.py
@@ -23,7 +23,7 @@
 LIST = NY * CAP
 TILE = 4
 ENTRIES = NX * LIST // TILE
-PAIR = 4
+PAIR = 2
 STATS = 16
 NEGATIVE = -1e30
 FLOOR = -1e29
@@ -79,15 +79,16 @@
     return stats[0:1] + stats[1:2] + stats[2:3]
 
 
-def attend_kernel(home, x, core, lists, new_kv, *rest):
-    shards, asked, rest = rest[:NY], rest[NY], rest[NY + 1:]
-    out, queries, fresh, held, peak, total, weighted, order, sems = rest
-    first = [pltpu.make_async_copy(asked, queries, sems.at[NY])]
+def attend_kernel(home, x, core, lists, queries, *rest):
     if home:
-        first.append(pltpu.make_async_copy(new_kv, fresh, sems.at[NY + 1]))
-    later = [pltpu.make_async_copy(shards[s], held.at[pl.ds(s * SLOTS, SLOTS)], sems.at[s]) for s in range(NY)]
-    for copy in first + later:
+        held, new_kv, out, fresh, peak, total, weighted, order, sems = rest
+        copies = [pltpu.make_async_copy(new_kv, fresh, sems.at[0])]
+    else:
+        shards, (out, held, peak, total, weighted, order, sems) = rest[:NY], rest[NY:]
+        copies = [pltpu.make_async_copy(shards[s], held.at[pl.ds(s * SLOTS, SLOTS)], sems.at[s]) for s in range(NY)]
+    for copy in copies:
         copy.start()
+
     def heads(g):
         q = queries[g]
         return jnp.concatenate([q[:, h * HD:(h + 1) * HD] for h in range(PER)], axis=0)
@@ -121,15 +122,13 @@
     for p in range(PAIR):
         order[used + p] = ENTRIES
 
-    for copy in first:
+    for copy in copies:
         copy.wait()
     if home:
         scores = contract(fresh[0], heads(x[0]), 1, 1)
         key = lax.broadcasted_iota(jnp.int32, (TOK, ROWS), 0)
         token = lax.broadcasted_iota(jnp.int32, (TOK, ROWS), 1) % TOK
         merge(x[0], *reduce(jnp.where(key <= token, scores, NEGATIVE), fresh[1]))
-    for copy in later:
-        copy.wait()
 
     def some_tiles(i, carry):
         results = []
@@ -162,27 +161,26 @@
     lax.fori_loop(0, NX, finish, 0)
 
 
-def attend(home, x, core, lists, new_kv, asked, shards):
+def attend(home, x, core, lists, asked, arrays):
     vmem, smem, free = (pl.BlockSpec(memory_space=m) for m in (pltpu.VMEM, pltpu.SMEM, pl.ANY))
-    new_kv, own = (pltpu.with_memory_space_constraint(a, pltpu.HBM) for a in (new_kv, shards[0]))
+    result = jax.ShapeDtypeStruct((NX, HD + STATS, ROWS), jnp.bfloat16)
+    blocks = (NY * SLOTS, 2, BLOCK, HD)
     return pl.pallas_call(
         functools.partial(attend_kernel, home),
-        out_shape=jax.ShapeDtypeStruct((NX, HD + STATS, ROWS), jnp.bfloat16),
-        in_specs=[smem, smem, smem] + [free] * (2 + NY),
-        out_specs=vmem,
-        scratch_shapes=[
-            pltpu.VMEM((NX, TOK, ROWS), jnp.bfloat16),
-            pltpu.VMEM((2, TOK, HD), jnp.bfloat16),
-            pltpu.VMEM((NY * SLOTS, 2, BLOCK, HD), jnp.bfloat16),
+        out_shape=result if home else [result, pltpu.VMEM(blocks, jnp.bfloat16)],
+        in_specs=[smem, smem, smem, vmem] + ([vmem, free] if home else [free] * NY),
+        out_specs=vmem if home else [vmem, vmem],
+        scratch_shapes=([pltpu.VMEM((2, TOK, HD), jnp.bfloat16)] if home else [])
+        + [
             pltpu.VMEM((NX, 1, ROWS), jnp.float32),
             pltpu.VMEM((NX, 1, ROWS), jnp.float32),
             pltpu.VMEM((NX, HD, ROWS), jnp.float32),
             pltpu.SMEM((ENTRIES + PAIR,), jnp.int32),
-            pltpu.SemaphoreType.DMA((NY + 2,)),
+            pltpu.SemaphoreType.DMA((NY,)),
         ],
         compiler_params=pltpu.CompilerParams(vmem_limit_bytes=16 << 20),
         name="attend_home" if home else "attend_other",
-    )(x, core, lists, new_kv, own, *shards[1:], asked)
+    )(x, core, lists, asked, *arrays)
 
 
 def combine_kernel(one, two, out):
@@ -269,10 +267,10 @@
     x, y, c = (lax.axis_index(name).reshape(1) for name in ("x", "y", "c"))
     shards, asked = spread(cache, queries)
     lists = block_lists(x, y, c, prefix_blocks, block_owner, block_slot)
-    other = attend(False, x, 1 - c, lists, new_kv, asked[1], shards)
-    lists, other = lax.optimization_barrier((lists, other))
+    new_kv, own = (pltpu.with_memory_space_constraint(a, pltpu.HBM) for a in (new_kv, shards[0]))
+    other, held = attend(False, x, 1 - c, lists, asked[1], [own, *shards[1:]])
     returned = lax.ppermute(other, "c", [(0, 1), (1, 0)])
-    parts = combine(attend(True, x, c, lists, new_kv, asked[0], shards), returned)
+    parts = combine(attend(True, x, c, lists, asked[0], [held, new_kv]), returned)
     parts = lax.all_to_all(parts, "x", split_axis=0, concat_axis=0, tiled=True)
     partial = project(parts, out_weight).reshape(NZ, TOK // NZ, -1)
     arrived = lax.all_to_all(partial, "z", split_axis=0, concat_axis=0, tiled=True)

time: 115 us -> 116 us (level)
  the two profiles are of different devices: /device:TPU:1 before, /device:TPU:24 now
where the time goes in v5:
time: 116 us; the launch traced here: 115 us
  blocking collectives  67.9 us (59%)
  starting transfers between devices  31.5 us (27%)
  Pallas kernels  14.2 us (12%)
    all_to_all x1, blocking collectives, local(): lax.all_to_all(partial, 'z', split_axis=0, concat_axis=0, tiled=True)  39.2 us
    ppermute x7, starting transfers between devices, shift(): return lax.ppermute(a, ('y', 'c'), pairs)  27.6 us
    all_gather x1, blocking collectives, spread(): same = lax.all_gather(queries, 'x', axis=0)  14.6 us
    all_to_all x1, blocking collectives, local(): parts = lax.all_to_all(parts, 'x', split_axis=0, concat_axis=0, tiled=True)  14.1 us
    pallas_call x2, Pallas kernels, attend(): pl.pallas_call(functools.partial(attend_kernel, home), out_shape=result i...  11.1 us
  transfers between devices with their start and end apart: 9, of which 1 were waited for; matrix products, arithmetic and copies ran while one was open for 0% of the time, Pallas kernels for 5%

profile of v5, /device:TPU:24, one launch (start us, length us, event | category | flops | bytes accessed | tf_op | source)
XLA Modules:
  0.0 115.4 jit_solution(991403303742392029)
XLA Ops:
  0.0 4.8 %collective-permute-start.2 = (bf16[8,2,64,128]{3,2,1,0:T(8,128)(2,1)}, bf16[8,2,64,128]{3,2,1,0:T(8,128)(2,1)S(1)}, u32[]{:S(2)}, u32[]{:S(2)}) collective-permute-start(bf16[8,2,64,128]{3,2,1,0:T(8,128)(2,1)} %rest_0_.1), channel_id=1, source_target_pairs={{0,32},{8,104},{16,48},{24,120},{32,64},{40,8},{48,80},{56,24},{64... | collective-permute-start | bytes 786440 | tf_op jit(solution)/shard_map/ppermute | solution.py:254
  4.8 1.9 %collective-permute-start.5 = (bf16[8,2,64,128]{3,2,1,0:T(8,128)(2,1)}, bf16[8,2,64,128]{3,2,1,0:T(8,128)(2,1)S(1)}, u32[]{:S(2)}, u32[]{:S(2)}) collective-permute-start(bf16[8,2,64,128]{3,2,1,0:T(8,128)(2,1)} %rest_0_.1), channel_id=1, source_target_pairs={{0,96},{8,40},{16,112},{24,56},{32,0},{40,72},{48,16},{56,88},{64,... | collective-permute-start | bytes 786440 | tf_op jit(solution)/shard_map/ppermute | solution.py:254
  6.8 5.2 %collective-permute-start.1 = (bf16[8,2,64,128]{3,2,1,0:T(8,128)(2,1)}, bf16[8,2,64,128]{3,2,1,0:T(8,128)(2,1)S(1)}, u32[]{:S(2)}, u32[]{:S(2)}) collective-permute-start(bf16[8,2,64,128]{3,2,1,0:T(8,128)(2,1)} %rest_0_.1), channel_id=1, source_target_pairs={{0,112},{8,24},{16,0},{24,40},{32,16},{40,56},{48,32},{56,72},{64,... | collective-permute-start | bytes 786440 | tf_op jit(solution)/shard_map/ppermute | solution.py:254
  11.9 2.7 %collective-permute-start = (bf16[8,2,64,128]{3,2,1,0:T(8,128)(2,1)}, bf16[8,2,64,128]{3,2,1,0:T(8,128)(2,1)S(1)}, u32[]{:S(2)}, u32[]{:S(2)}) collective-permute-start(bf16[8,2,64,128]{3,2,1,0:T(8,128)(2,1)} %rest_0_.1), channel_id=1, source_target_pairs={{0,16},{8,120},{16,32},{24,8},{32,48},{40,24},{48,64},{56,40},{64,... | collective-permute-start | bytes 786440 | tf_op jit(solution)/shard_map/ppermute | solution.py:254
  14.6 0.0 collective-permute-done.2.rest_6_
  14.6 7.8 %collective-permute-start.4 = (bf16[8,2,64,128]{3,2,1,0:T(8,128)(2,1)S(1)}, bf16[8,2,64,128]{3,2,1,0:T(8,128)(2,1)S(1)}, u32[]{:S(2)}, u32[]{:S(2)}) collective-permute-start(bf16[8,2,64,128]{3,2,1,0:T(8,128)(2,1)S(1)} %collective-permute-done.2.rest_6_), channel_id=1, source_target_pairs={{0,16},{8,120},{16,32},{24,8},{32,48},{40,24},{48,64},{56,40},{64,... | collective-permute-start | bytes 786440 | tf_op jit(solution)/shard_map/ppermute | solution.py:254
  22.4 3.3 %collective-permute-start.3 = (bf16[8,2,64,128]{3,2,1,0:T(8,128)(2,1)S(1)}, bf16[8,2,64,128]{3,2,1,0:T(8,128)(2,1)S(1)}, u32[]{:S(2)}, u32[]{:S(2)}) collective-permute-start(bf16[8,2,64,128]{3,2,1,0:T(8,128)(2,1)S(1)} %collective-permute-done.2.rest_6_), channel_id=1, source_target_pairs={{0,32},{8,104},{16,48},{24,120},{32,64},{40,8},{48,80},{56,24},{64... | collective-permute-start | bytes 786440 | tf_op jit(solution)/shard_map/ppermute | solution.py:254
  25.7 0.0 collective-permute-done.5.rest_2_
  25.7 2.0 %collective-permute-start.6 = (bf16[8,2,64,128]{3,2,1,0:T(8,128)(2,1)S(1)}, bf16[8,2,64,128]{3,2,1,0:T(8,128)(2,1)S(1)}, u32[]{:S(2)}, u32[]{:S(2)}) collective-permute-start(bf16[8,2,64,128]{3,2,1,0:T(8,128)(2,1)S(1)} %collective-permute-done.5.rest_2_), channel_id=1, source_target_pairs={{0,112},{8,24},{16,0},{24,40},{32,16},{40,56},{48,32},{56,72},{64,... | collective-permute-start | bytes 786440 | tf_op jit(solution)/shard_map/ppermute | solution.py:254
  27.7 14.6 %all-gather = bf16[512,512]{1,0:T(8,128)(2,1)S(1)} all-gather(bf16[128,512]{1,0:T(8,128)(2,1)} %param.7), channel_id=2, replica_groups=mesh['x'=4,'y'=8,'c'=2,'z'=8] {'x'}, dimensions={0}, use_global_device_ids=true | all-gather | bytes 655360 | tf_op jit(solution)/shard_map/all_gather | solution.py:259
  42.3 0.0 collective-permute-done.1.rest_1_
  42.3 0.0 collective-permute-done.rest_7_
  42.3 0.0 collective-permute-done.4.rest_5_
  42.3 0.0 collective-permute-done.3.rest_4_
  42.3 0.0 collective-permute-done.6.rest_3_
  42.3 1.9 %collective-permute-start.7 = (bf16[4,128,512]{2,1,0:T(8,128)(2,1)S(1)}, bf16[4,128,512]{2,1,0:T(8,128)(2,1)S(1)}, u32[]{:S(2)}, u32[]{:S(2)}) collective-permute-start(bf16[4,128,512]{2,1,0:T(8,128)(2,1)S(1)} %bitcast.6), channel_id=1, source_target_pairs={{0,8},{8,0},{1,9},{9,1},{2,10},{10,2},{3,11},{11,3},{4,12},{12,4},... | collective-permute-start | bytes 1572872 | tf_op jit(solution)/shard_map/ppermute | solution.py:262
  44.3 0.0 copy-start.1
  44.3 0.6 copy-done.1
  44.9 1.0 block_lists.1.lists
  45.9 0.0 copy-start
  46.0 0.2 collective-permute-done.7.queries
  46.1 6.4 %attend_other.1 = (bf16[4,144,512]{2,1,0:T(8,128)(2,1)S(1)}, bf16[64,2,64,128]{3,2,1,0:T(8,128)(2,1)S(1)}) custom-call(s32[1]{0:T(128)} %bitcast.x, s32[1]{0:T(128)S(6)} %sub.3.core, s32[8,128]{1,0:T(8,128)S(1)} %block_lists.1.lists, bf16[4,128,512]{2,1,0:T(8,128)(2,1)S(1)} %collective-permute-done.7.queries, bf16[8,2,64,128]{3,2,1,0:T(8,128)(2,1)} %rest_0_.1, ...), custom_call_target="tpu_custom_call" | custom-call | tf_op jit(solution)/shard_map/attend_other/pallas_call | solution.py:168
  52.6 1.9 %collective-permute-start.8 = (bf16[4,144,512]{2,1,0:T(8,128)(2,1)S(1)}, bf16[4,144,512]{2,1,0:T(8,128)(2,1)S(1)}, u32[]{:S(2)}, u32[]{:S(2)}) collective-permute-start(bf16[4,144,512]{2,1,0:T(8,128)(2,1)S(1)} %get-tuple-element.20), channel_id=1, source_target_pairs={{0,8},{8,0},{1,9},{9,1},{2,10},{10,2},{3,11},{11,3},{4,12},{12,4},... | collective-permute-start | bytes 1769480 | tf_op jit(solution)/shard_map/ppermute | solution.py:272
  54.5 4.7 %attend_home.1.one = bf16[4,144,512]{2,1,0:T(8,128)(2,1)S(1)} custom-call(s32[1]{0:T(128)} %bitcast.x, s32[1]{0:T(128)} %bitcast.1.c.core, s32[8,128]{1,0:T(8,128)S(1)} %block_lists.1.lists, bf16[4,128,512]{2,1,0:T(8,128)(2,1)S(1)} %bitcast.7, bf16[64,2,64,128]{3,2,1,0:T(8,128)(2,1)S(1)} %get-tuple-element.19.rest_0_, bf16[2,128,128]{2,1,0:T(8,128)(2,1)} %rest_1_.1), custom_call_target="tpu_custom_call" | custom-call | tf_op jit(solution)/shard_map/attend_home/pallas_call | solution.py:168
  59.2 0.0 collective-permute-done.8.two
  59.2 0.3 combine.1
  59.5 14.1 %all_to_all.10.parts = bf16[4,144,512]{2,1,0:T(8,128)(2,1)S(1)} all-to-all(bf16[4,144,512]{2,1,0:T(8,128)(2,1)S(1)} %combine.1), channel_id=1, replica_groups=mesh['x'=4,'y'=8,'c'=2,'z'=8] {'x'}, dimensions={0} | all-to-all | bytes 1179648 | tf_op jit(solution)/shard_map/all_to_all | solution.py:274
  73.6 0.0 copy-done
  73.6 1.8 %project.1 = bf16[128,4096]{1,0:T(8,128)(2,1)S(1)} custom-call(bf16[4,144,512]{2,1,0:T(8,128)(2,1)S(1)} %all_to_all.10.parts, bf16[512,4096]{1,0:T(8,128)(2,1)S(1)} %copy-done), custom_call_target="tpu_custom_call" | custom-call | tf_op jit(solution)/shard_map/project/pallas_call | solution.py:236
  75.4 39.2 %all_to_all.11 = bf16[8,16,4096]{2,1,0:T(8,128)(2,1)S(1)} all-to-all(bf16[8,16,4096]{2,1,0:T(8,128)(2,1)S(1)} %bitcast.5), channel_id=1, replica_groups=mesh['x'=4,'y'=8,'c'=2,'z'=8] {'z'}, dimensions={0} | all-to-all | bytes 2097152 | tf_op jit(solution)/shard_map/all_to_all | solution.py:276
  114.6 0.8 reduce_sum.12
Async XLA Ops:
  0.0 14.6 %collective-permute-start.2 = (bf16[8,2,64,128]{3,2,1,0:T(8,128)(2,1)}, bf16[8,2,64,128]{3,2,1,0:T(8,128)(2,1)S(1)}, u32[]{:S(2)}, u32[]{:S(2)}) collective-permute-start(bf16[8,2,64,128]{3,2,1,0:T(8,128)(2,1)} %rest_0_.1), channel_id=1, source_target_pairs={{0,32},{8,104},{16,48},{24,120},{32,64},{40,8},{48,80},{56,24},{64... | collective-permute-start | bytes 786440 | tf_op jit(solution)/shard_map/ppermute | solution.py:254
  4.8 20.9 %collective-permute-start.5 = (bf16[8,2,64,128]{3,2,1,0:T(8,128)(2,1)}, bf16[8,2,64,128]{3,2,1,0:T(8,128)(2,1)S(1)}, u32[]{:S(2)}, u32[]{:S(2)}) collective-permute-start(bf16[8,2,64,128]{3,2,1,0:T(8,128)(2,1)} %rest_0_.1), channel_id=1, source_target_pairs={{0,96},{8,40},{16,112},{24,56},{32,0},{40,72},{48,16},{56,88},{64,... | collective-permute-start | bytes 786440 | tf_op jit(solution)/shard_map/ppermute | solution.py:254
  6.8 35.5 %collective-permute-start.1 = (bf16[8,2,64,128]{3,2,1,0:T(8,128)(2,1)}, bf16[8,2,64,128]{3,2,1,0:T(8,128)(2,1)S(1)}, u32[]{:S(2)}, u32[]{:S(2)}) collective-permute-start(bf16[8,2,64,128]{3,2,1,0:T(8,128)(2,1)} %rest_0_.1), channel_id=1, source_target_pairs={{0,112},{8,24},{16,0},{24,40},{32,16},{40,56},{48,32},{56,72},{64,... | collective-permute-start | bytes 786440 | tf_op jit(solution)/shard_map/ppermute | solution.py:254
  11.9 30.4 %collective-permute-start = (bf16[8,2,64,128]{3,2,1,0:T(8,128)(2,1)}, bf16[8,2,64,128]{3,2,1,0:T(8,128)(2,1)S(1)}, u32[]{:S(2)}, u32[]{:S(2)}) collective-permute-start(bf16[8,2,64,128]{3,2,1,0:T(8,128)(2,1)} %rest_0_.1), channel_id=1, source_target_pairs={{0,16},{8,120},{16,32},{24,8},{32,48},{40,24},{48,64},{56,40},{64,... | collective-permute-start | bytes 786440 | tf_op jit(solution)/shard_map/ppermute | solution.py:254
  14.6 27.7 %collective-permute-start.4 = (bf16[8,2,64,128]{3,2,1,0:T(8,128)(2,1)S(1)}, bf16[8,2,64,128]{3,2,1,0:T(8,128)(2,1)S(1)}, u32[]{:S(2)}, u32[]{:S(2)}) collective-permute-start(bf16[8,2,64,128]{3,2,1,0:T(8,128)(2,1)S(1)} %collective-permute-done.2.rest_6_), channel_id=1, source_target_pairs={{0,16},{8,120},{16,32},{24,8},{32,48},{40,24},{48,64},{56,40},{64,... | collective-permute-start | bytes 786440 | tf_op jit(solution)/shard_map/ppermute | solution.py:254
  22.4 19.9 %collective-permute-start.3 = (bf16[8,2,64,128]{3,2,1,0:T(8,128)(2,1)S(1)}, bf16[8,2,64,128]{3,2,1,0:T(8,128)(2,1)S(1)}, u32[]{:S(2)}, u32[]{:S(2)}) collective-permute-start(bf16[8,2,64,128]{3,2,1,0:T(8,128)(2,1)S(1)} %collective-permute-done.2.rest_6_), channel_id=1, source_target_pairs={{0,32},{8,104},{16,48},{24,120},{32,64},{40,8},{48,80},{56,24},{64... | collective-permute-start | bytes 786440 | tf_op jit(solution)/shard_map/ppermute | solution.py:254
  25.7 16.6 %collective-permute-start.6 = (bf16[8,2,64,128]{3,2,1,0:T(8,128)(2,1)S(1)}, bf16[8,2,64,128]{3,2,1,0:T(8,128)(2,1)S(1)}, u32[]{:S(2)}, u32[]{:S(2)}) collective-permute-start(bf16[8,2,64,128]{3,2,1,0:T(8,128)(2,1)S(1)} %collective-permute-done.5.rest_2_), channel_id=1, source_target_pairs={{0,112},{8,24},{16,0},{24,40},{32,16},{40,56},{48,32},{56,72},{64,... | collective-permute-start | bytes 786440 | tf_op jit(solution)/shard_map/ppermute | solution.py:254
  42.3 3.8 %collective-permute-start.7 = (bf16[4,128,512]{2,1,0:T(8,128)(2,1)S(1)}, bf16[4,128,512]{2,1,0:T(8,128)(2,1)S(1)}, u32[]{:S(2)}, u32[]{:S(2)}) collective-permute-start(bf16[4,128,512]{2,1,0:T(8,128)(2,1)S(1)} %bitcast.6), channel_id=1, source_target_pairs={{0,8},{8,0},{1,9},{9,1},{2,10},{10,2},{3,11},{11,3},{4,12},{12,4},... | collective-permute-start | bytes 1572872 | tf_op jit(solution)/shard_map/ppermute | solution.py:262
  44.3 0.7 copy-start.1
  45.9 27.7 %copy-start = (bf16[512,4096]{1,0:T(8,128)(2,1)S(1)}, bf16[512,4096]{1,0:T(8,128)(2,1)}, u32[]{:S(2)}) copy-start(bf16[512,4096]{1,0:T(8,128)(2,1)} %weight.1) | copy-start | bytes 12582916
  52.6 6.6 %collective-permute-start.8 = (bf16[4,144,512]{2,1,0:T(8,128)(2,1)S(1)}, bf16[4,144,512]{2,1,0:T(8,128)(2,1)S(1)}, u32[]{:S(2)}, u32[]{:S(2)}) collective-permute-start(bf16[4,144,512]{2,1,0:T(8,128)(2,1)S(1)} %get-tuple-element.20), channel_id=1, source_target_pairs={{0,8},{8,0},{1,9},{9,1},{2,10},{10,2},{3,11},{11,3},{4,12},{12,4},... | collective-permute-start | bytes 1769480 | tf_op jit(solution)/shard_map/ppermute | solution.py:272

commit v6 on v5

--- a/solution.py
+++ b/solution.py
@@ -63,7 +63,7 @@
         out_specs=vmem,
         compiler_params=pltpu.CompilerParams(vmem_limit_bytes=4 << 20),
         name="block_lists",
-    )(x, y, c, lengths, *(pltpu.with_memory_space_constraint(a, pltpu.HBM) for a in (owners, slots)))
+    )(x, y, c, *(pltpu.with_memory_space_constraint(a, pltpu.HBM) for a in (lengths, owners, slots)))
 
 
 def split_level(level):

time: 116 us -> 116 us (level)
  the two profiles are of different devices: /device:TPU:24 before, /device:TPU:16 now
where the time goes in v6:
time: 116 us
  blocking collectives  68.6 us (59%)
  starting transfers between devices  29.7 us (26%)
  Pallas kernels  12.1 us (10%)
  waiting for transfers between devices  4.45 us (4%)
    all_to_all x1, blocking collectives, local(): lax.all_to_all(partial, 'z', split_axis=0, concat_axis=0, tiled=True)  39.1 us
    ppermute x7, starting transfers between devices, shift(): return lax.ppermute(a, ('y', 'c'), pairs)  25.6 us
    all_to_all x1, blocking collectives, local(): parts = lax.all_to_all(parts, 'x', split_axis=0, concat_axis=0, tiled=True)  15.6 us
    all_gather x1, blocking collectives, spread(): same = lax.all_gather(queries, 'x', axis=0)  13.9 us
    pallas_call x2, Pallas kernels, attend(): pl.pallas_call(functools.partial(attend_kernel, home), out_shape=result i...  8.99 us
    ppermute x7, waiting for transfers between devices, shift(): return lax.ppermute(a, ('y', 'c'), pairs)  3.6 us
  transfers between devices with their start and end apart: 9, of which 2 were waited for; matrix products, arithmetic and copies ran while one was open for 0% of the time, Pallas kernels for 5%

profile of v6, /device:TPU:16, one launch (start us, length us, event | category | flops | bytes accessed | tf_op | source)
XLA Modules:
  0.0 115.9 jit_solution(13167476471302244523)
XLA Ops:
  0.0 5.7 %collective-permute-start.2 = (bf16[8,2,64,128]{3,2,1,0:T(8,128)(2,1)}, bf16[8,2,64,128]{3,2,1,0:T(8,128)(2,1)S(1)}, u32[]{:S(2)}, u32[]{:S(2)}) collective-permute-start(bf16[8,2,64,128]{3,2,1,0:T(8,128)(2,1)} %rest_0_.1), channel_id=1, source_target_pairs={{0,32},{8,104},{16,48},{24,120},{32,64},{40,8},{48,80},{56,24},{64... | collective-permute-start | bytes 786440 | tf_op jit(solution)/shard_map/ppermute | solution.py:254
  5.7 3.8 %collective-permute-start.5 = (bf16[8,2,64,128]{3,2,1,0:T(8,128)(2,1)}, bf16[8,2,64,128]{3,2,1,0:T(8,128)(2,1)S(1)}, u32[]{:S(2)}, u32[]{:S(2)}) collective-permute-start(bf16[8,2,64,128]{3,2,1,0:T(8,128)(2,1)} %rest_0_.1), channel_id=1, source_target_pairs={{0,96},{8,40},{16,112},{24,56},{32,0},{40,72},{48,16},{56,88},{64,... | collective-permute-start | bytes 786440 | tf_op jit(solution)/shard_map/ppermute | solution.py:254
  9.5 1.9 %collective-permute-start.1 = (bf16[8,2,64,128]{3,2,1,0:T(8,128)(2,1)}, bf16[8,2,64,128]{3,2,1,0:T(8,128)(2,1)S(1)}, u32[]{:S(2)}, u32[]{:S(2)}) collective-permute-start(bf16[8,2,64,128]{3,2,1,0:T(8,128)(2,1)} %rest_0_.1), channel_id=1, source_target_pairs={{0,112},{8,24},{16,0},{24,40},{32,16},{40,56},{48,32},{56,72},{64,... | collective-permute-start | bytes 786440 | tf_op jit(solution)/shard_map/ppermute | solution.py:254
  11.5 3.9 %collective-permute-start = (bf16[8,2,64,128]{3,2,1,0:T(8,128)(2,1)}, bf16[8,2,64,128]{3,2,1,0:T(8,128)(2,1)S(1)}, u32[]{:S(2)}, u32[]{:S(2)}) collective-permute-start(bf16[8,2,64,128]{3,2,1,0:T(8,128)(2,1)} %rest_0_.1), channel_id=1, source_target_pairs={{0,16},{8,120},{16,32},{24,8},{32,48},{40,24},{48,64},{56,40},{64,... | collective-permute-start | bytes 786440 | tf_op jit(solution)/shard_map/ppermute | solution.py:254
  15.4 3.6 %collective-permute-done.2.rest_6_ = bf16[8,2,64,128]{3,2,1,0:T(8,128)(2,1)S(1)} collective-permute-done((bf16[8,2,64,128]{3,2,1,0:T(8,128)(2,1)}, bf16[8,2,64,128]{3,2,1,0:T(8,128)(2,1)S(1)}, u32[]{:S(2)}, u32[]{:S(2)}) %collective-permute-start.2) | collective-permute-done | bytes 262176 | tf_op jit(solution)/shard_map/ppermute | solution.py:254
  19.0 1.9 %collective-permute-start.4 = (bf16[8,2,64,128]{3,2,1,0:T(8,128)(2,1)S(1)}, bf16[8,2,64,128]{3,2,1,0:T(8,128)(2,1)S(1)}, u32[]{:S(2)}, u32[]{:S(2)}) collective-permute-start(bf16[8,2,64,128]{3,2,1,0:T(8,128)(2,1)S(1)} %collective-permute-done.2.rest_6_), channel_id=1, source_target_pairs={{0,16},{8,120},{16,32},{24,8},{32,48},{40,24},{48,64},{56,40},{64,... | collective-permute-start | bytes 786440 | tf_op jit(solution)/shard_map/ppermute | solution.py:254
  20.9 4.4 %collective-permute-start.3 = (bf16[8,2,64,128]{3,2,1,0:T(8,128)(2,1)S(1)}, bf16[8,2,64,128]{3,2,1,0:T(8,128)(2,1)S(1)}, u32[]{:S(2)}, u32[]{:S(2)}) collective-permute-start(bf16[8,2,64,128]{3,2,1,0:T(8,128)(2,1)S(1)} %collective-permute-done.2.rest_6_), channel_id=1, source_target_pairs={{0,32},{8,104},{16,48},{24,120},{32,64},{40,8},{48,80},{56,24},{64... | collective-permute-start | bytes 786440 | tf_op jit(solution)/shard_map/ppermute | solution.py:254
  25.3 0.0 collective-permute-done.5.rest_2_
  25.3 3.9 %collective-permute-start.6 = (bf16[8,2,64,128]{3,2,1,0:T(8,128)(2,1)S(1)}, bf16[8,2,64,128]{3,2,1,0:T(8,128)(2,1)S(1)}, u32[]{:S(2)}, u32[]{:S(2)}) collective-permute-start(bf16[8,2,64,128]{3,2,1,0:T(8,128)(2,1)S(1)} %collective-permute-done.5.rest_2_), channel_id=1, source_target_pairs={{0,112},{8,24},{16,0},{24,40},{32,16},{40,56},{48,32},{56,72},{64,... | collective-permute-start | bytes 786440 | tf_op jit(solution)/shard_map/ppermute | solution.py:254
  29.3 13.9 %all-gather = bf16[512,512]{1,0:T(8,128)(2,1)S(1)} all-gather(bf16[128,512]{1,0:T(8,128)(2,1)} %param.7), channel_id=2, replica_groups=mesh['x'=4,'y'=8,'c'=2,'z'=8] {'x'}, dimensions={0}, use_global_device_ids=true | all-gather | bytes 655360 | tf_op jit(solution)/shard_map/all_gather | solution.py:259
  43.2 0.0 collective-permute-done.1.rest_1_
  43.2 0.0 collective-permute-done.rest_7_
  43.2 0.0 collective-permute-done.4.rest_5_
  43.2 0.0 collective-permute-done.3.rest_4_
  43.2 0.0 collective-permute-done.6.rest_3_
  43.2 1.9 %collective-permute-start.7 = (bf16[4,128,512]{2,1,0:T(8,128)(2,1)S(1)}, bf16[4,128,512]{2,1,0:T(8,128)(2,1)S(1)}, u32[]{:S(2)}, u32[]{:S(2)}) collective-permute-start(bf16[4,128,512]{2,1,0:T(8,128)(2,1)S(1)} %bitcast.6), channel_id=1, source_target_pairs={{0,8},{8,0},{1,9},{9,1},{2,10},{10,2},{3,11},{11,3},{4,12},{12,4},... | collective-permute-start | bytes 1572872 | tf_op jit(solution)/shard_map/ppermute | solution.py:262
  45.2 1.0 block_lists.1.lists
  46.2 0.0 copy-start
  46.2 0.8 collective-permute-done.7.queries
  47.0 4.4 %attend_other.1 = (bf16[4,144,512]{2,1,0:T(8,128)(2,1)S(1)}, bf16[64,2,64,128]{3,2,1,0:T(8,128)(2,1)S(1)}) custom-call(s32[1]{0:T(128)} %bitcast.x, s32[1]{0:T(128)S(6)} %sub.3.core, s32[8,128]{1,0:T(8,128)S(1)} %block_lists.1.lists, bf16[4,128,512]{2,1,0:T(8,128)(2,1)S(1)} %collective-permute-done.7.queries, bf16[8,2,64,128]{3,2,1,0:T(8,128)(2,1)} %rest_0_.1, ...), custom_call_target="tpu_custom_call" | custom-call | tf_op jit(solution)/shard_map/attend_other/pallas_call | solution.py:168
  51.4 2.2 %collective-permute-start.8 = (bf16[4,144,512]{2,1,0:T(8,128)(2,1)S(1)}, bf16[4,144,512]{2,1,0:T(8,128)(2,1)S(1)}, u32[]{:S(2)}, u32[]{:S(2)}) collective-permute-start(bf16[4,144,512]{2,1,0:T(8,128)(2,1)S(1)} %get-tuple-element.20), channel_id=1, source_target_pairs={{0,8},{8,0},{1,9},{9,1},{2,10},{10,2},{3,11},{11,3},{4,12},{12,4},... | collective-permute-start | bytes 1769480 | tf_op jit(solution)/shard_map/ppermute | solution.py:272
  53.6 4.6 %attend_home.1.one = bf16[4,144,512]{2,1,0:T(8,128)(2,1)S(1)} custom-call(s32[1]{0:T(128)} %bitcast.x, s32[1]{0:T(128)} %bitcast.1.c.core, s32[8,128]{1,0:T(8,128)S(1)} %block_lists.1.lists, bf16[4,128,512]{2,1,0:T(8,128)(2,1)S(1)} %bitcast.7, bf16[64,2,64,128]{3,2,1,0:T(8,128)(2,1)S(1)} %get-tuple-element.19.rest_0_, bf16[2,128,128]{2,1,0:T(8,128)(2,1)} %rest_1_.1), custom_call_target="tpu_custom_call" | custom-call | tf_op jit(solution)/shard_map/attend_home/pallas_call | solution.py:168
  58.2 0.0 collective-permute-done.8.two
  58.3 0.3 combine.1
  58.6 15.6 %all_to_all.10.parts = bf16[4,144,512]{2,1,0:T(8,128)(2,1)S(1)} all-to-all(bf16[4,144,512]{2,1,0:T(8,128)(2,1)S(1)} %combine.1), channel_id=1, replica_groups=mesh['x'=4,'y'=8,'c'=2,'z'=8] {'x'}, dimensions={0} | all-to-all | bytes 1179648 | tf_op jit(solution)/shard_map/all_to_all | solution.py:274
  74.1 0.0 copy-done
  74.1 1.8 %project.1 = bf16[128,4096]{1,0:T(8,128)(2,1)S(1)} custom-call(bf16[4,144,512]{2,1,0:T(8,128)(2,1)S(1)} %all_to_all.10.parts, bf16[512,4096]{1,0:T(8,128)(2,1)S(1)} %copy-done), custom_call_target="tpu_custom_call" | custom-call | tf_op jit(solution)/shard_map/project/pallas_call | solution.py:236
  76.0 39.1 %all_to_all.11 = bf16[8,16,4096]{2,1,0:T(8,128)(2,1)S(1)} all-to-all(bf16[8,16,4096]{2,1,0:T(8,128)(2,1)S(1)} %bitcast.5), channel_id=1, replica_groups=mesh['x'=4,'y'=8,'c'=2,'z'=8] {'z'}, dimensions={0} | all-to-all | bytes 2097152 | tf_op jit(solution)/shard_map/all_to_all | solution.py:276
  115.1 0.8 reduce_sum.12
Async XLA Ops:
  0.0 19.0 %collective-permute-start.2 = (bf16[8,2,64,128]{3,2,1,0:T(8,128)(2,1)}, bf16[8,2,64,128]{3,2,1,0:T(8,128)(2,1)S(1)}, u32[]{:S(2)}, u32[]{:S(2)}) collective-permute-start(bf16[8,2,64,128]{3,2,1,0:T(8,128)(2,1)} %rest_0_.1), channel_id=1, source_target_pairs={{0,32},{8,104},{16,48},{24,120},{32,64},{40,8},{48,80},{56,24},{64... | collective-permute-start | bytes 786440 | tf_op jit(solution)/shard_map/ppermute | solution.py:254
  5.7 19.6 %collective-permute-start.5 = (bf16[8,2,64,128]{3,2,1,0:T(8,128)(2,1)}, bf16[8,2,64,128]{3,2,1,0:T(8,128)(2,1)S(1)}, u32[]{:S(2)}, u32[]{:S(2)}) collective-permute-start(bf16[8,2,64,128]{3,2,1,0:T(8,128)(2,1)} %rest_0_.1), channel_id=1, source_target_pairs={{0,96},{8,40},{16,112},{24,56},{32,0},{40,72},{48,16},{56,88},{64,... | collective-permute-start | bytes 786440 | tf_op jit(solution)/shard_map/ppermute | solution.py:254
  9.5 33.6 %collective-permute-start.1 = (bf16[8,2,64,128]{3,2,1,0:T(8,128)(2,1)}, bf16[8,2,64,128]{3,2,1,0:T(8,128)(2,1)S(1)}, u32[]{:S(2)}, u32[]{:S(2)}) collective-permute-start(bf16[8,2,64,128]{3,2,1,0:T(8,128)(2,1)} %rest_0_.1), channel_id=1, source_target_pairs={{0,112},{8,24},{16,0},{24,40},{32,16},{40,56},{48,32},{56,72},{64,... | collective-permute-start | bytes 786440 | tf_op jit(solution)/shard_map/ppermute | solution.py:254
  11.5 31.7 %collective-permute-start = (bf16[8,2,64,128]{3,2,1,0:T(8,128)(2,1)}, bf16[8,2,64,128]{3,2,1,0:T(8,128)(2,1)S(1)}, u32[]{:S(2)}, u32[]{:S(2)}) collective-permute-start(bf16[8,2,64,128]{3,2,1,0:T(8,128)(2,1)} %rest_0_.1), channel_id=1, source_target_pairs={{0,16},{8,120},{16,32},{24,8},{32,48},{40,24},{48,64},{56,40},{64,... | collective-permute-start | bytes 786440 | tf_op jit(solution)/shard_map/ppermute | solution.py:254
  19.0 24.2 %collective-permute-start.4 = (bf16[8,2,64,128]{3,2,1,0:T(8,128)(2,1)S(1)}, bf16[8,2,64,128]{3,2,1,0:T(8,128)(2,1)S(1)}, u32[]{:S(2)}, u32[]{:S(2)}) collective-permute-start(bf16[8,2,64,128]{3,2,1,0:T(8,128)(2,1)S(1)} %collective-permute-done.2.rest_6_), channel_id=1, source_target_pairs={{0,16},{8,120},{16,32},{24,8},{32,48},{40,24},{48,64},{56,40},{64,... | collective-permute-start | bytes 786440 | tf_op jit(solution)/shard_map/ppermute | solution.py:254
  20.9 22.3 %collective-permute-start.3 = (bf16[8,2,64,128]{3,2,1,0:T(8,128)(2,1)S(1)}, bf16[8,2,64,128]{3,2,1,0:T(8,128)(2,1)S(1)}, u32[]{:S(2)}, u32[]{:S(2)}) collective-permute-start(bf16[8,2,64,128]{3,2,1,0:T(8,128)(2,1)S(1)} %collective-permute-done.2.rest_6_), channel_id=1, source_target_pairs={{0,32},{8,104},{16,48},{24,120},{32,64},{40,8},{48,80},{56,24},{64... | collective-permute-start | bytes 786440 | tf_op jit(solution)/shard_map/ppermute | solution.py:254
  25.3 17.9 %collective-permute-start.6 = (bf16[8,2,64,128]{3,2,1,0:T(8,128)(2,1)S(1)}, bf16[8,2,64,128]{3,2,1,0:T(8,128)(2,1)S(1)}, u32[]{:S(2)}, u32[]{:S(2)}) collective-permute-start(bf16[8,2,64,128]{3,2,1,0:T(8,128)(2,1)S(1)} %collective-permute-done.5.rest_2_), channel_id=1, source_target_pairs={{0,112},{8,24},{16,0},{24,40},{32,16},{40,56},{48,32},{56,72},{64,... | collective-permute-start | bytes 786440 | tf_op jit(solution)/shard_map/ppermute | solution.py:254
  43.2 3.8 %collective-permute-start.7 = (bf16[4,128,512]{2,1,0:T(8,128)(2,1)S(1)}, bf16[4,128,512]{2,1,0:T(8,128)(2,1)S(1)}, u32[]{:S(2)}, u32[]{:S(2)}) collective-permute-start(bf16[4,128,512]{2,1,0:T(8,128)(2,1)S(1)} %bitcast.6), channel_id=1, source_target_pairs={{0,8},{8,0},{1,9},{9,1},{2,10},{10,2},{3,11},{11,3},{4,12},{12,4},... | collective-permute-start | bytes 1572872 | tf_op jit(solution)/shard_map/ppermute | solution.py:262
  46.2 28.0 %copy-start = (bf16[512,4096]{1,0:T(8,128)(2,1)S(1)}, bf16[512,4096]{1,0:T(8,128)(2,1)}, u32[]{:S(2)}) copy-start(bf16[512,4096]{1,0:T(8,128)(2,1)} %weight.1) | copy-start | bytes 12582916
  51.4 6.9 %collective-permute-start.8 = (bf16[4,144,512]{2,1,0:T(8,128)(2,1)S(1)}, bf16[4,144,512]{2,1,0:T(8,128)(2,1)S(1)}, u32[]{:S(2)}, u32[]{:S(2)}) collective-permute-start(bf16[4,144,512]{2,1,0:T(8,128)(2,1)S(1)} %get-tuple-element.20), channel_id=1, source_target_pairs={{0,8},{8,0},{1,9},{9,1},{2,10},{10,2},{3,11},{11,3},{4,12},{12,4},... | collective-permute-start | bytes 1769480 | tf_op jit(solution)/shard_map/ppermute | solution.py:272
